TPU v7x, 128 devices: a whole 4x4x4 slice. The times are simulated.
128 devices in a mesh: row: 16 (over z_lo, y, core), col: 8 (over z_hi, x).
Axes of the slice: x: 4, y: 4, z: 4 (z_hi: 2, z_lo: 2; z = z_hi * 2 + z_lo), core: 2. Of those that a mesh axis runs over, the one named last changes fastest.
Arguments:
- coords: float32 [16, 65536], P(None, ('row', 'col')), may hold values from -6 to 6
- lengthscale: float32 [16], replicated, may hold values from 1.5 to 3
- solution: float32 [64, 65536], P(None, ('row', 'col')), may hold values from -6 to 6
- residual: float32 [64, 65536], P(None, ('row', 'col')), may hold values from -6 to 6
- direction: float32 [64, 65536], P(None, ('row', 'col')), may hold values from -6 to 6
Outputs:
- new_solution: float32 [64, 65536], P(None, ('row', 'col'))
- new_residual: float32 [64, 65536], P(None, ('row', 'col'))
- new_direction: float32 [64, 65536], P(None, ('row', 'col'))
All inputs are finite; a program needn't handle non-finite values.
Results may differ from a plain program's by a relative error of at most 0.0054.
Values may be sent and summed in bfloat16 or wider, within the bound.
A program may use at most 64 MiB of HBM per device.

v0:
```python
import math

import jax
import jax.numpy as jnp
from jax import lax
from jax.sharding import PartitionSpec as P


def matern(col_scaled, row_scaled, row_sq):
    col_sq = jnp.sum(col_scaled.astype(jnp.float32) ** 2, axis=0)
    cross = lax.dot_general(
        col_scaled, row_scaled, (((0,), (0,)), ((), ())), preferred_element_type=jnp.float32
    )
    dist2 = jnp.maximum(col_sq[:, None] + row_sq[None, :] - 2.0 * cross, 0.0)
    radius = jnp.sqrt(dist2)
    root_five = math.sqrt(5.0)
    value = (1.0 + root_five * radius + 5.0 / 3.0 * dist2) * jnp.exp(-root_five * radius)
    return value.astype(jnp.bfloat16)


def accumulate(running, col_scaled, col_dir, row_scaled, row_sq):
    extent = col_scaled.shape[1]
    block = math.gcd(extent, 512)
    count = extent // block

    def advance(index, partial_value):
        piece_scaled = lax.dynamic_slice_in_dim(col_scaled, index * block, block, 1)
        piece_dir = lax.dynamic_slice_in_dim(col_dir, index * block, block, 1)
        kern = matern(piece_scaled, row_scaled, row_sq)
        return partial_value + jnp.dot(piece_dir, kern, preferred_element_type=jnp.float32)

    return lax.fori_loop(0, count, advance, running)


def local(coords, lengthscale, solution, residual, direction):
    scaled = (coords / lengthscale[:, None]).astype(jnp.bfloat16)
    dir_half = direction.astype(jnp.bfloat16)
    norm_old = lax.psum(jnp.sum(residual * residual, axis=1), ("row", "col"))
    row_scaled = lax.all_gather(scaled, "col", axis=1, tiled=True)
    row_sq = jnp.sum(row_scaled.astype(jnp.float32) ** 2, axis=0)
    empty = jnp.zeros((dir_half.shape[0], row_scaled.shape[1]), jnp.float32)
    col_scaled, col_dir = (
        lax.all_gather(scaled, "row", axis=1, tiled=True),
        lax.all_gather(dir_half, "row", axis=1, tiled=True),
    )
    result = accumulate(empty, col_scaled, col_dir, row_scaled, row_sq)
    image = lax.psum_scatter(result, "col", scatter_dimension=1, tiled=True) + direction
    curv = lax.psum(jnp.sum(direction * image, axis=1), ("row", "col"))
    alpha = norm_old / curv
    new_solution = solution + alpha[:, None] * direction
    new_residual = residual - alpha[:, None] * image
    fresh = lax.psum(jnp.sum(new_residual * new_residual, axis=1), ("row", "col"))
    new_direction = new_residual + (fresh / norm_old)[:, None] * direction
    return (new_solution, new_residual, new_direction)


def solution(mesh):
    in_specs = (
        P(None, ("row", "col")),
        P(),
        P(None, ("row", "col")),
        P(None, ("row", "col")),
        P(None, ("row", "col")),
    )
    out_specs = (P(None, ("row", "col")), P(None, ("row", "col")), P(None, ("row", "col")))
    return jax.shard_map(local, mesh=mesh, in_specs=in_specs, out_specs=out_specs, check_vma=False)
```

profile of v0, /device:TPU:1, one launch (start us, length us, event | category | flops | bytes accessed | tf_op | source)
XLA Modules:
  0.0 383.1 jit_solution(5968825282319553465)
XLA Ops:
  7.2 0.0 all-gather.2.cloned.1.call-start
  7.2 1.5 convert_element_type.23
  8.8 0.0 all-gather.2.cloned.1.call-update
  8.8 0.0 reduce-scatter.2.cloned.1.call-start
  8.8 0.8 divide_convert_fusion
  9.7 29.9 %all_gather.11 = bf16[16,4096]{1,0:T(8,128)(2,1)S(1)} all-gather(bf16[16,512]{1,0:T(8,128)(2,1)S(1)} %divide_convert_fusion), channel_id=1, replica_groups=mesh['row'=16,'col'=8] {'col'}, dimensions={1}, use_global_device_ids=true | all-gather | bytes 147456 | tf_op jit(solution)/shard_map/all_gather | solution.py:39
  39.6 0.1 multiply_reduce_fusion.1
  39.6 27.2 %all_gather.10 = bf16[16,8192]{1,0:T(8,128)(2,1)S(1)} all-gather(bf16[16,512]{1,0:T(8,128)(2,1)S(1)} %divide_convert_fusion), channel_id=1, replica_groups=mesh['row'=16,'col'=8] {'row'}, dimensions={1}, use_global_device_ids=true | all-gather | bytes 278528 | tf_op jit(solution)/shard_map/all_gather | solution.py:43
  66.9 0.0 all-gather.2.cloned.1.call-done
  66.9 109.1 %while.14 = (s32[]{:T(128)}, f32[64,4096]{1,0:T(8,128)S(1)}, bf16[64,8192]{1,0:T(8,128)(2,1)}, bf16[16,8192]{1,0:T(8,128)(2,1)S(1)}, f32[4096]{0:T(1024)S(1)}, /...) while((s32[]{:T(128)}, f32[64,4096]{1,0:T(8,128)S(1)}, ...), condition=%wide.region_5.0_spmd.clone, body=%wide.region_3.0_spmd.clone.sunk | while | flops 359161344 | bytes 2348704 | solution.py:32
  66.9 6.8 %convolution_add_fusion.2 = f32[64,4096]{1,0:T(8,128)S(1)} fusion(bf16[16,4096]{1,0:T(8,128)(2,1)S(1)} %get-tuple-element.216, f32[4096]{0:T(1024)S(1)} %get-tuple-element.215, f32[512]{0:T(512)S(1)} %multiply_reduce_fusion.6, f32[64,4096]{1,0:T(8,128)S(1)} %get-tuple-element.202, pred[]{:T(512)S(6)} %compare.3, ...), kind=kOutput, calls=%fused_computation.1.clone.1 | convolution fusion | flops 359137280 | bytes 2330112 | tf_op jit(solution)/shard_map/while/body/eval_jaxpr/dot_general | solution.py:30
  73.7 6.8 %convolution_add_fusion.2 = f32[64,4096]{1,0:T(8,128)S(1)} fusion(bf16[16,4096]{1,0:T(8,128)(2,1)S(1)} %get-tuple-element.216, f32[4096]{0:T(1024)S(1)} %get-tuple-element.215, f32[512]{0:T(512)S(1)} %multiply_reduce_fusion.6, f32[64,4096]{1,0:T(8,128)S(1)} %get-tuple-element.202, pred[]{:T(512)S(6)} %compare.3, ...), kind=kOutput, calls=%fused_computation.1.clone.1 | convolution fusion | flops 359137280 | bytes 2330112 | tf_op jit(solution)/shard_map/while/body/eval_jaxpr/dot_general | solution.py:30
  80.5 6.8 %convolution_add_fusion.2 = f32[64,4096]{1,0:T(8,128)S(1)} fusion(bf16[16,4096]{1,0:T(8,128)(2,1)S(1)} %get-tuple-element.216, f32[4096]{0:T(1024)S(1)} %get-tuple-element.215, f32[512]{0:T(512)S(1)} %multiply_reduce_fusion.6, f32[64,4096]{1,0:T(8,128)S(1)} %get-tuple-element.202, pred[]{:T(512)S(6)} %compare.3, ...), kind=kOutput, calls=%fused_computation.1.clone.1 | convolution fusion | flops 359137280 | bytes 2330112 | tf_op jit(solution)/shard_map/while/body/eval_jaxpr/dot_general | solution.py:30
  87.3 6.8 %convolution_add_fusion.2 = f32[64,4096]{1,0:T(8,128)S(1)} fusion(bf16[16,4096]{1,0:T(8,128)(2,1)S(1)} %get-tuple-element.216, f32[4096]{0:T(1024)S(1)} %get-tuple-element.215, f32[512]{0:T(512)S(1)} %multiply_reduce_fusion.6, f32[64,4096]{1,0:T(8,128)S(1)} %get-tuple-element.202, pred[]{:T(512)S(6)} %compare.3, ...), kind=kOutput, calls=%fused_computation.1.clone.1 | convolution fusion | flops 359137280 | bytes 2330112 | tf_op jit(solution)/shard_map/while/body/eval_jaxpr/dot_general | solution.py:30
  94.2 6.8 %convolution_add_fusion.2 = f32[64,4096]{1,0:T(8,128)S(1)} fusion(bf16[16,4096]{1,0:T(8,128)(2,1)S(1)} %get-tuple-element.216, f32[4096]{0:T(1024)S(1)} %get-tuple-element.215, f32[512]{0:T(512)S(1)} %multiply_reduce_fusion.6, f32[64,4096]{1,0:T(8,128)S(1)} %get-tuple-element.202, pred[]{:T(512)S(6)} %compare.3, ...), kind=kOutput, calls=%fused_computation.1.clone.1 | convolution fusion | flops 359137280 | bytes 2330112 | tf_op jit(solution)/shard_map/while/body/eval_jaxpr/dot_general | solution.py:30
  101.0 6.8 %convolution_add_fusion.2 = f32[64,4096]{1,0:T(8,128)S(1)} fusion(bf16[16,4096]{1,0:T(8,128)(2,1)S(1)} %get-tuple-element.216, f32[4096]{0:T(1024)S(1)} %get-tuple-element.215, f32[512]{0:T(512)S(1)} %multiply_reduce_fusion.6, f32[64,4096]{1,0:T(8,128)S(1)} %get-tuple-element.202, pred[]{:T(512)S(6)} %compare.3, ...), kind=kOutput, calls=%fused_computation.1.clone.1 | convolution fusion | flops 359137280 | bytes 2330112 | tf_op jit(solution)/shard_map/while/body/eval_jaxpr/dot_general | solution.py:30
  107.8 6.8 %convolution_add_fusion.2 = f32[64,4096]{1,0:T(8,128)S(1)} fusion(bf16[16,4096]{1,0:T(8,128)(2,1)S(1)} %get-tuple-element.216, f32[4096]{0:T(1024)S(1)} %get-tuple-element.215, f32[512]{0:T(512)S(1)} %multiply_reduce_fusion.6, f32[64,4096]{1,0:T(8,128)S(1)} %get-tuple-element.202, pred[]{:T(512)S(6)} %compare.3, ...), kind=kOutput, calls=%fused_computation.1.clone.1 | convolution fusion | flops 359137280 | bytes 2330112 | tf_op jit(solution)/shard_map/while/body/eval_jaxpr/dot_general | solution.py:30
  114.6 6.8 %convolution_add_fusion.2 = f32[64,4096]{1,0:T(8,128)S(1)} fusion(bf16[16,4096]{1,0:T(8,128)(2,1)S(1)} %get-tuple-element.216, f32[4096]{0:T(1024)S(1)} %get-tuple-element.215, f32[512]{0:T(512)S(1)} %multiply_reduce_fusion.6, f32[64,4096]{1,0:T(8,128)S(1)} %get-tuple-element.202, pred[]{:T(512)S(6)} %compare.3, ...), kind=kOutput, calls=%fused_computation.1.clone.1 | convolution fusion | flops 359137280 | bytes 2330112 | tf_op jit(solution)/shard_map/while/body/eval_jaxpr/dot_general | solution.py:30
  121.5 6.8 %convolution_add_fusion.2 = f32[64,4096]{1,0:T(8,128)S(1)} fusion(bf16[16,4096]{1,0:T(8,128)(2,1)S(1)} %get-tuple-element.216, f32[4096]{0:T(1024)S(1)} %get-tuple-element.215, f32[512]{0:T(512)S(1)} %multiply_reduce_fusion.6, f32[64,4096]{1,0:T(8,128)S(1)} %get-tuple-element.202, pred[]{:T(512)S(6)} %compare.3, ...), kind=kOutput, calls=%fused_computation.1.clone.1 | convolution fusion | flops 359137280 | bytes 2330112 | tf_op jit(solution)/shard_map/while/body/eval_jaxpr/dot_general | solution.py:30
  128.3 6.8 %convolution_add_fusion.2 = f32[64,4096]{1,0:T(8,128)S(1)} fusion(bf16[16,4096]{1,0:T(8,128)(2,1)S(1)} %get-tuple-element.216, f32[4096]{0:T(1024)S(1)} %get-tuple-element.215, f32[512]{0:T(512)S(1)} %multiply_reduce_fusion.6, f32[64,4096]{1,0:T(8,128)S(1)} %get-tuple-element.202, pred[]{:T(512)S(6)} %compare.3, ...), kind=kOutput, calls=%fused_computation.1.clone.1 | convolution fusion | flops 359137280 | bytes 2330112 | tf_op jit(solution)/shard_map/while/body/eval_jaxpr/dot_general | solution.py:30
  135.1 6.8 %convolution_add_fusion.2 = f32[64,4096]{1,0:T(8,128)S(1)} fusion(bf16[16,4096]{1,0:T(8,128)(2,1)S(1)} %get-tuple-element.216, f32[4096]{0:T(1024)S(1)} %get-tuple-element.215, f32[512]{0:T(512)S(1)} %multiply_reduce_fusion.6, f32[64,4096]{1,0:T(8,128)S(1)} %get-tuple-element.202, pred[]{:T(512)S(6)} %compare.3, ...), kind=kOutput, calls=%fused_computation.1.clone.1 | convolution fusion | flops 359137280 | bytes 2330112 | tf_op jit(solution)/shard_map/while/body/eval_jaxpr/dot_general | solution.py:30
  141.9 6.8 %convolution_add_fusion.2 = f32[64,4096]{1,0:T(8,128)S(1)} fusion(bf16[16,4096]{1,0:T(8,128)(2,1)S(1)} %get-tuple-element.216, f32[4096]{0:T(1024)S(1)} %get-tuple-element.215, f32[512]{0:T(512)S(1)} %multiply_reduce_fusion.6, f32[64,4096]{1,0:T(8,128)S(1)} %get-tuple-element.202, pred[]{:T(512)S(6)} %compare.3, ...), kind=kOutput, calls=%fused_computation.1.clone.1 | convolution fusion | flops 359137280 | bytes 2330112 | tf_op jit(solution)/shard_map/while/body/eval_jaxpr/dot_general | solution.py:30
  148.7 6.8 %convolution_add_fusion.2 = f32[64,4096]{1,0:T(8,128)S(1)} fusion(bf16[16,4096]{1,0:T(8,128)(2,1)S(1)} %get-tuple-element.216, f32[4096]{0:T(1024)S(1)} %get-tuple-element.215, f32[512]{0:T(512)S(1)} %multiply_reduce_fusion.6, f32[64,4096]{1,0:T(8,128)S(1)} %get-tuple-element.202, pred[]{:T(512)S(6)} %compare.3, ...), kind=kOutput, calls=%fused_computation.1.clone.1 | convolution fusion | flops 359137280 | bytes 2330112 | tf_op jit(solution)/shard_map/while/body/eval_jaxpr/dot_general | solution.py:30
  155.6 6.8 %convolution_add_fusion.2 = f32[64,4096]{1,0:T(8,128)S(1)} fusion(bf16[16,4096]{1,0:T(8,128)(2,1)S(1)} %get-tuple-element.216, f32[4096]{0:T(1024)S(1)} %get-tuple-element.215, f32[512]{0:T(512)S(1)} %multiply_reduce_fusion.6, f32[64,4096]{1,0:T(8,128)S(1)} %get-tuple-element.202, pred[]{:T(512)S(6)} %compare.3, ...), kind=kOutput, calls=%fused_computation.1.clone.1 | convolution fusion | flops 359137280 | bytes 2330112 | tf_op jit(solution)/shard_map/while/body/eval_jaxpr/dot_general | solution.py:30
  162.4 6.8 %convolution_add_fusion.2 = f32[64,4096]{1,0:T(8,128)S(1)} fusion(bf16[16,4096]{1,0:T(8,128)(2,1)S(1)} %get-tuple-element.216, f32[4096]{0:T(1024)S(1)} %get-tuple-element.215, f32[512]{0:T(512)S(1)} %multiply_reduce_fusion.6, f32[64,4096]{1,0:T(8,128)S(1)} %get-tuple-element.202, pred[]{:T(512)S(6)} %compare.3, ...), kind=kOutput, calls=%fused_computation.1.clone.1 | convolution fusion | flops 359137280 | bytes 2330112 | tf_op jit(solution)/shard_map/while/body/eval_jaxpr/dot_general | solution.py:30
  169.2 6.8 %convolution_add_fusion.2 = f32[64,4096]{1,0:T(8,128)S(1)} fusion(bf16[16,4096]{1,0:T(8,128)(2,1)S(1)} %get-tuple-element.216, f32[4096]{0:T(1024)S(1)} %get-tuple-element.215, f32[512]{0:T(512)S(1)} %multiply_reduce_fusion.6, f32[64,4096]{1,0:T(8,128)S(1)} %get-tuple-element.202, pred[]{:T(512)S(6)} %compare.3, ...), kind=kOutput, calls=%fused_computation.1.clone.1 | convolution fusion | flops 359137280 | bytes 2330112 | tf_op jit(solution)/shard_map/while/body/eval_jaxpr/dot_general | solution.py:30
  176.0 0.0 copy-start.1
  176.0 0.0 copy-start.3
  176.0 0.0 copy-start
  176.0 0.0 copy-start.4
  176.0 0.9 copy-done.1
  177.0 0.0 reduce-scatter.2.cloned.1.call-update
  177.0 0.0 copy-done.3
  177.0 0.1 multiply_reduce_fusion.4
  177.1 68.4 %reduce-scatter.2.cloned.1.call-done = f32[64,512]{1,0:T(8,128)} async-done(((f32[64,4096]{1,0:T(8,128)}), f32[64,512]{1,0:T(8,128)}) %reduce-scatter.2.cloned.1.call-update) | async-done | bytes 131088 | tf_op jit(solution)/shard_map/reduce_scatter | solution.py:47
  245.5 0.0 copy-done
  245.6 1.0 multiply_reduce_fusion.3
  246.6 66.1 %all-reduce = (f32[64]{0:T(128)S(1)}, f32[64]{0:T(128)S(1)}) all-reduce(f32[64]{0:T(128)S(1)} %multiply_reduce_fusion.4, f32[64]{0:T(128)S(1)} %get-tuple-element.150), channel_id=1, replica_groups=mesh['row'=16,'col'=8] {'row','col'}, use_global_device_ids=true, to_apply=%region_1.0 | all-reduce | flops 128 | bytes 1024 | tf_op jit(solution)/shard_map/psum | solution.py:38
  312.7 0.2 multiply_reduce_fusion.2
  312.9 0.0 copy-start.2
  312.9 62.5 %psum.23 = f32[64]{0:T(128)S(1)} all-reduce(f32[64]{0:T(128)S(1)} %get-tuple-element.148), channel_id=1, replica_groups=mesh['row'=16,'col'=8] {'row','col'}, use_global_device_ids=true, to_apply=%region_10.0 | all-reduce | flops 64 | bytes 512 | tf_op jit(solution)/shard_map/psum | solution.py:52
  375.5 0.0 copy-done.4
  375.5 0.8 multiply_add_fusion
  376.3 0.0 copy-done.2
  (19 shorter events, 0.4 us)
Async XLA Ops:
  7.2 59.7 %all-gather.2.cloned.1.call-start = ((), (), s32[]{:S(2)}) async-start(), calls=%async_computation.1 | async-start | bytes 1114112 | tf_op jit(solution)/shard_map/all_gather | solution.py:44
  8.8 236.8 %reduce-scatter.2.cloned.1.call-start = ((), (), s32[]{:S(2)}) async-start(), calls=%async_computation.2 | async-start | bytes 1179648 | tf_op jit(solution)/shard_map/reduce_scatter | solution.py:47
  176.0 1.0 copy-start.1
  176.0 1.0 copy-start.3
  176.0 69.6 %copy-start = (f32[64,512]{1,0:T(8,128)S(1)}, f32[64,512]{1,0:T(8,128)}, u32[]{:S(2)}) copy-start(f32[64,512]{1,0:T(8,128)} %param.11) | copy-start | bytes 393220
  176.0 199.5 %copy-start.4 = (f32[64,512]{1,0:T(8,128)S(1)}, f32[64,512]{1,0:T(8,128)}, u32[]{:S(2)}) copy-start(f32[64,512]{1,0:T(8,128)} %param.9) | copy-start | bytes 393220
  312.9 63.4 %copy-start.2 = (f32[64,512]{1,0:T(8,128)}, f32[64,512]{1,0:T(8,128)S(1)}, u32[]{:S(2)}) copy-start(f32[64,512]{1,0:T(8,128)S(1)} %get-tuple-element.149) | copy-start | bytes 393220
Sparse Core Ops, SparseCore 0:
  10.2 36.0 all-gather.1
  177.1 68.3 reduce-scatter.1
where the time goes:
time: 384 us; the launch traced here: 383 us
  blocking collectives  186 us (48%)
  matrix products  108 us (28%)
  waiting for transfers between devices  68.4 us (18%)
  between operations  14.1 us (4%)
  other arithmetic  4.99 us (1%)
    dot_general x16, matrix products, advance(): jnp.dot(piece_dir, kern, preferred_element_type=jnp.float32)  108 us
    reduce_scatter x1, waiting for transfers between devices, local(): lax.psum_scatter(result, 'col', scatter_dimension=1, tiled=True) + direction  68.4 us
    psum x1, blocking collectives, local(): norm_old = lax.psum(jnp.sum(residual * residual, axis=1), ('row', 'col'))  66.1 us
    psum x1, blocking collectives, local(): lax.psum(jnp.sum(new_residual * new_residual, axis=1), ('row', 'col'))  62.5 us
    all_gather x1, blocking collectives, local(): row_scaled = lax.all_gather(scaled, 'col', axis=1, tiled=True)  29.9 us
    all_gather x1, blocking collectives, local(): lax.all_gather(scaled, 'row', axis=1, tiled=True)  27.2 us
  transfers between devices with their start and end apart: 2, of which 1 were waited for; matrix products, arithmetic and copies ran while one was open for 0% of the time, Pallas kernels for 0%

commit v1 on v0

v1 whole, which is shorter than its diff:
```python
import math

import jax
import jax.numpy as jnp
from jax import lax
from jax.experimental import pallas as pl
from jax.experimental.pallas import tpu as pltpu
from jax.sharding import PartitionSpec as P

MESH = pl.DeviceIdType.MESH
F32 = jnp.float32
BF16 = jnp.bfloat16

NS = 8
NT = 8
NDEV = 128
HALF = 4
FEAT = 32
LN2 = math.log(2.0)
SCALE = 5.0 / LN2**2
SHIFT = 1.5 / LN2
CONST = 0.75 / LN2**2
FACTOR = LN2**2 / 3.0 * 2.0**SHIFT
WIDTH = 256


def entries(x):
    t = jnp.maximum(x, 1e-12)
    w = -SHIFT - t * lax.rsqrt(t)
    return ((w * w + CONST) * jnp.exp2(w)).astype(BF16)


def pieces(value):
    high = value.astype(BF16).astype(F32)
    mid = (value - high).astype(BF16).astype(F32)
    low = (value - high - mid).astype(BF16).astype(F32)
    return high, mid, low


def kernel(
    coords, scale, solution, residual, direction, new_solution, new_residual, new_direction,
    blk, left, right, dir_s, acc_s, acc_t, out, got, x0, x1, k0, k1, mine, part, one, two,
    blk_send, blk_recv, out_send, out_recv, one_send, one_recv, two_send, two_recv,
):
    ncol = NS
    me = lax.axis_index("row") * ncol + lax.axis_index("col")

    def device(offset):
        label = lax.rem(me + offset + NDEV, NDEV)
        return (label // ncol, lax.rem(label, ncol))

    def block_copy(slot, offset):
        return pltpu.make_async_remote_copy(
            src_ref=blk.at[0], dst_ref=blk.at[slot], send_sem=blk_send.at[slot], recv_sem=blk_recv.at[slot],
            device_id=device(offset), device_id_type=MESH,
        )

    def s_copy(s):
        return block_copy(s, -s)

    def t_copy(t):
        return block_copy(NS - 1 + t, -8 * t)

    def out_copy(slot, offset):
        return pltpu.make_async_remote_copy(
            src_ref=out.at[slot], dst_ref=got.at[slot], send_sem=out_send.at[slot], recv_sem=out_recv.at[slot],
            device_id=device(offset), device_id_type=MESH,
        )

    barrier = pltpu.get_barrier_semaphore()
    for s in range(1, NS):
        pl.semaphore_signal(barrier, inc=1, device_id=device(s), device_id_type=MESH)
        pl.semaphore_signal(barrier, inc=1, device_id=device(-s), device_id_type=MESH)
    for t in range(1, 16):
        pl.semaphore_signal(barrier, inc=1, device_id=device(8 * t), device_id_type=MESH)

    scaled = (coords[...] / scale[...]).astype(BF16)
    wide = scaled.astype(F32)
    sq = jnp.sum(wide * wide, axis=0, keepdims=True)
    high, mid, low = pieces(sq)
    rows = lax.broadcasted_iota(jnp.int32, (16, sq.shape[1]), 0)
    extra = jnp.where(rows == 0, high, jnp.where(rows == 1, mid, jnp.where(rows == 2, low, 0.0)))
    extra = jnp.where((rows >= 8) & (rows < 11), 1.0, extra)
    blk[0, 0:16, :] = scaled
    blk[0, 16:32, :] = extra.astype(BF16)
    blk[0, 32:96, :] = direction[...].astype(BF16)

    pl.semaphore_wait(barrier, 29)
    t_copy(1).start()
    for s in range(1, HALF):
        s_copy(s).start()
    for t in range(2, 5):
        t_copy(t).start()
    for s in range(HALF, NS):
        s_copy(s).start()
    for t in range(5, NT + 1):
        t_copy(t).start()

    def prepare_s(s):
        wide = blk[s, 0:32, :].astype(F32)
        turned = jnp.concatenate([wide[0:16] * (-2.0 * SCALE), wide[24:32] * SCALE, wide[16:24] * SCALE], axis=0)
        high, mid, low = pieces(turned)
        right[s, 0:32, :] = high.astype(BF16)
        right[s, 32:64, :] = mid.astype(BF16)
        right[s, 64:96, :] = low.astype(BF16)
        dir_s[s] = blk[s, 32:96, :]

    def prepare_t(slot):
        wide = blk[slot, 0:32, :].astype(F32)
        four = jnp.concatenate([wide, wide, wide, jnp.zeros_like(wide)], axis=0)
        left[...] = four.T.astype(BF16)

    def cross(x, s, half):
        for j in range(0, 512, WIDTH):
            x[j : j + WIDTH, :] = lax.dot_general(
                left[j : j + WIDTH, 0:96], right[s, :, half * WIDTH : (half + 1) * WIDTH],
                (((1,), (0,)), ((), ())), preferred_element_type=F32,
            )

    def fill(k, x):
        for j in range(0, 512, WIDTH):
            k[j : j + WIDTH, :] = entries(x[j : j + WIDTH, :])

    def add_s(k, s, half, slot):
        cols = slice(half * WIDTH, (half + 1) * WIDTH)
        acc_s[s, :, cols] += lax.dot_general(
            blk[slot, 32:96, :], k[...], (((1,), (0,)), ((), ())), preferred_element_type=F32
        )

    def add_t(k, s, half):
        cols = slice(half * WIDTH, (half + 1) * WIDTH)
        acc_t[...] += lax.dot_general(
            dir_s[s, :, cols], k[...], (((1,), (1,)), ((), ())), preferred_element_type=F32
        )

    acc_s[...] = jnp.zeros_like(acc_s)
    prepare_s(0)
    prepare_t(0)
    for half, (x, k) in enumerate(((x0, k0), (x1, k1))):
        cross(x, 0, half)
        fill(k, x)
        add_s(k, 0, half, 0)

    xs, ks = (x0, x1), (k0, k1)
    groups = HALF * 2

    def strip(h, t):
        slot = NS - 1 + t
        prepare_t(slot)
        acc_t[...] = jnp.zeros_like(acc_t)
        for g in range(groups + 2):
            if g < groups:
                cross(xs[g % 2], h * HALF + g // 2, g % 2)
            if g >= 2:
                add_s(ks[g % 2], h * HALF + (g - 2) // 2, g % 2, slot)
                add_t(ks[g % 2], h * HALF + (g - 2) // 2, g % 2)
            if 1 <= g <= groups:
                fill(ks[(g - 1) % 2], xs[(g - 1) % 2])

    def outer(h, carry):
        @pl.when(h == 0)
        def _():
            for s in range(1, HALF):
                s_copy(s).wait_recv()
                prepare_s(s)

        @pl.when(h == 1)
        def _():
            for s in range(1, HALF):
                out[s - 1] = acc_s[s].astype(BF16)
                out_copy(s - 1, s).start()
            for s in range(HALF, NS):
                s_copy(s).wait_recv()
                prepare_s(s)

        def inner(t, carry):
            @pl.when(h == 0)
            def _():
                t_copy(t).wait_recv()

                @pl.when(t == NT)
                def _():
                    dir_s[0] = jnp.zeros_like(dir_s[0])

            strip(h, t)

            @pl.when(h == 0)
            def _():
                part[t - 1] = acc_t[...]

            @pl.when(h == 1)
            def _():
                out[NS - 2 + t] = (acc_t[...] + part[t - 1]).astype(BF16)
                out_copy(NS - 2 + t, 8 * t).start()

            return carry

        return lax.fori_loop(1, NT + 1, inner, carry)

    lax.fori_loop(0, 2, outer, 0)
    for s in range(HALF, NS):
        out[s - 1] = acc_s[s].astype(BF16)
        out_copy(s - 1, s).start()

    res, dirn = residual[...], direction[...]
    total = acc_s[0]
    for slot in (0, 1, 2, 7, 8, 9, 10, 11, 12, 13, 3, 4, 5, 6, 14):
        out_copy(slot, 0).wait_recv()
        total = total + got[slot].astype(F32)
    image = total * FACTOR + dirn
    new_residual[...] = image

    def lanes(value):
        return jnp.sum(value, axis=1, keepdims=True)

    lane = lax.broadcasted_iota(jnp.int32, (64, 128), 1)
    table = jnp.where(lane == 0, lanes(res * res), 0.0)
    table = jnp.where(lane == 1, lanes(dirn * image), table)
    table = jnp.where(lane == 2, lanes(res * image), table)
    table = jnp.where(lane == 3, lanes(image * image), table)
    mine[...] = jnp.concatenate([table, jnp.zeros_like(table)], axis=0).T[0:8, :]

    def one_copy(s):
        return pltpu.make_async_remote_copy(
            src_ref=mine, dst_ref=one.at[s], send_sem=one_send.at[s], recv_sem=one_recv.at[s],
            device_id=device(-s), device_id_type=MESH,
        )

    def two_copy(t):
        return pltpu.make_async_remote_copy(
            src_ref=two.at[0], dst_ref=two.at[t], send_sem=two_send.at[t], recv_sem=two_recv.at[t],
            device_id=device(-8 * t), device_id_type=MESH,
        )

    for s in range(1, NS):
        one_copy(s).start()
    value = mine[...]
    for s in range(1, NS):
        one_copy(s).wait_recv()
        value = value + one[s]
    two[0] = value
    for t in range(1, 16):
        two_copy(t).start()
    for t in range(1, 16):
        two_copy(t).wait_recv()
        value = value + two[t]

    square = jnp.concatenate([value, jnp.zeros((120, 128), F32)], axis=0).T
    norm_old, curv = square[0:64, 0:1], square[0:64, 1:2]
    mixed, norm_image = square[0:64, 2:3], square[0:64, 3:4]
    alpha = norm_old / curv
    fresh = jnp.maximum(norm_old - alpha * (2.0 * mixed - alpha * norm_image), 0.0)
    beta = fresh / norm_old
    new_solution[...] = solution[...] + alpha * dirn
    updated = res - alpha * new_residual[...]
    new_residual[...] = updated
    new_direction[...] = updated + beta * dirn

    for s in range(1, NS):
        s_copy(s).wait_send()
        one_copy(s).wait_send()
    for t in range(1, NT + 1):
        t_copy(t).wait_send()
    for slot in range(15):
        out_copy(slot, 0).wait_send()
    for t in range(1, 16):
        two_copy(t).wait_send()


def local(coords, lengthscale, solution, residual, direction):
    probes, points = direction.shape
    big = jax.ShapeDtypeStruct((probes, points), F32)
    dma = pltpu.SemaphoreType.DMA
    return pl.pallas_call(
        kernel,
        out_shape=(big, big, big),
        in_specs=[pl.BlockSpec(memory_space=pltpu.VMEM)] * 5,
        out_specs=[pl.BlockSpec(memory_space=pltpu.VMEM)] * 3,
        scratch_shapes=[
            pltpu.VMEM((16, 96, 512), BF16),
            pltpu.VMEM((512, 128), BF16),
            pltpu.VMEM((NS, 96, 512), BF16),
            pltpu.VMEM((NS, 64, 512), BF16),
            pltpu.VMEM((NS, 64, 512), F32),
            pltpu.VMEM((64, 512), F32),
            pltpu.VMEM((15, 64, 512), BF16),
            pltpu.VMEM((15, 64, 512), BF16),
            pltpu.VMEM((512, WIDTH), F32),
            pltpu.VMEM((512, WIDTH), F32),
            pltpu.VMEM((512, WIDTH), BF16),
            pltpu.VMEM((512, WIDTH), BF16),
            pltpu.VMEM((8, 128), F32),
            pltpu.VMEM((NT, 64, 512), F32),
            pltpu.VMEM((NS, 8, 128), F32),
            pltpu.VMEM((16, 8, 128), F32),
            dma((16,)), dma((16,)), dma((15,)), dma((15,)), dma((8,)), dma((8,)), dma((16,)), dma((16,)),
        ],
        compiler_params=pltpu.CompilerParams(
            collective_id=0, has_side_effects=True, vmem_limit_bytes=48 * 2**20
        ),
    )(coords, lengthscale[:, None], solution, residual, direction)


def solution(mesh):
    spec = P(None, ("row", "col"))
    return jax.shard_map(
        local, mesh=mesh, in_specs=(spec, P(), spec, spec, spec), out_specs=(spec, spec, spec), check_vma=False
    )
```

time: 384 us -> 82.2 us (0.21)
  blocking collectives: 186 us -> 0 us
  matrix products: 108 us -> 0 us
  Pallas kernels: 0 us -> 75.1 us
  waiting for transfers between devices: 68.4 us -> 0 us
  between operations: 14.1 us -> 0.65 us
  local copies, waits for them, and re-layouts: 1.01 us -> 6.17 us
  other arithmetic: 4.99 us -> 0 us
    psum x2 -> x0, blocking collectives: 129 us -> none  [the longest x1 66.1 us: local(): norm_old = lax.psum(jnp.sum(residual * residual, axis=1), ('row', 'col'))]
    dot_general x16 -> x0, matrix products: 108 us -> none  [advance(): jnp.dot(piece_dir, kern, preferred_element_type=jnp.float32)]
    pallas_call x0 -> x1, Pallas kernels: none -> 75.1 us  [local(): pl.pallas_call(kernel, out_shape=(big, big, big), in_specs=[pl.BlockSpec(...]
    reduce_scatter x1 -> x0, waiting for transfers between devices: 68.4 us -> none  [local(): lax.psum_scatter(result, 'col', scatter_dimension=1, tiled=True) + direction]
    all_gather x2 -> x0, blocking collectives: 57.1 us -> none  [the longest x1 29.9 us: local(): row_scaled = lax.all_gather(scaled, 'col', axis=1, tiled=True)]
    unnamed x10 -> x13, local copies, waits for them, and re-layouts: 1.01 us -> 6.08 us
  transfers between devices with their start and end apart: 2 -> 0, of which waited for: 1 -> 0; matrix products, arithmetic and copies ran while one was open for 0% -> 0% of each run, Pallas kernels for 0% -> 0%
where the time goes in v1:
time: 82.2 us; the launch traced here: 82 us
  Pallas kernels  75.1 us (91%)
  local copies, waits for them, and re-layouts  6.17 us (8%)
    pallas_call x1, Pallas kernels, local(): pl.pallas_call(kernel, out_shape=(big, big, big), in_specs=[pl.BlockSpec(...  75.1 us
    unnamed x13, local copies, waits for them, and re-layouts  6.08 us

profile of v1, /device:TPU:1, one launch (start us, length us, event | category | flops | bytes accessed | tf_op | source)
XLA Modules:
  0.0 82.0 jit_solution(8193645725127597643)
XLA Ops:
  0.6 0.0 copy-start.4
  0.6 0.6 copy-done.4
  1.3 0.1 copy.8.scale
  1.4 0.0 copy-start
  1.4 0.9 %copy-done = f32[64,512]{1,0:T(8,128)S(1)} copy-done((f32[64,512]{1,0:T(8,128)S(1)}, f32[64,512]{1,0:T(8,128)}, u32[]{:S(2)}) %copy-start) | copy-done | bytes 131096
  2.3 0.0 copy-start.1
  2.3 0.9 %copy-done.1 = f32[64,512]{1,0:T(8,128)S(1)} copy-done((f32[64,512]{1,0:T(8,128)S(1)}, f32[64,512]{1,0:T(8,128)}, u32[]{:S(2)}) %copy-start.1) | copy-done | bytes 131096
  3.2 0.0 copy-start.2
  3.2 0.9 %copy-done.2 = f32[64,512]{1,0:T(8,128)S(1)} copy-done((f32[64,512]{1,0:T(8,128)S(1)}, f32[64,512]{1,0:T(8,128)}, u32[]{:S(2)}) %copy-start.2) | copy-done | bytes 131096
  4.1 0.0 copy-start.3
  4.1 0.8 copy-done.3
  4.8 75.1 %shard_map.76 = (f32[64,512]{1,0:T(8,128)S(1)}, f32[64,512]{1,0:T(8,128)S(1)}, f32[64,512]{1,0:T(8,128)S(1)}) custom-call(f32[16,512]{1,0:T(8,128)S(1)} %copy-done.3, f32[16,1]{1,0:T(8,128)S(1)} %copy.8.scale, f32[64,512]{1,0:T(8,128)S(1)} %copy-done, f32[64,512]{1,0:T(8,128)S(1)} %copy-done.1, f32[64,512]{1,0:T(8,128)S(1)} %copy-done.2), custom_call_target="tpu_custom_call" | custom-call | tf_op jit(solution)/shard_map/pallas_call | solution.py:274
  80.0 0.7 copy.12
  80.7 0.7 copy.13
  81.3 0.7 copy.14
Async XLA Ops:
  0.6 0.7 copy-start.4
  1.4 0.9 %copy-start = (f32[64,512]{1,0:T(8,128)S(1)}, f32[64,512]{1,0:T(8,128)}, u32[]{:S(2)}) copy-start(f32[64,512]{1,0:T(8,128)} %solution.1) | copy-start | bytes 393220
  2.3 0.9 %copy-start.1 = (f32[64,512]{1,0:T(8,128)S(1)}, f32[64,512]{1,0:T(8,128)}, u32[]{:S(2)}) copy-start(f32[64,512]{1,0:T(8,128)} %residual.1) | copy-start | bytes 393220
  3.2 0.9 %copy-start.2 = (f32[64,512]{1,0:T(8,128)S(1)}, f32[64,512]{1,0:T(8,128)}, u32[]{:S(2)}) copy-start(f32[64,512]{1,0:T(8,128)} %direction.1) | copy-start | bytes 393220
  4.1 0.8 copy-start.3

commit v2 on v1

v2 whole, which is shorter than its diff:
```python
import math

import jax
import jax.numpy as jnp
from jax import lax
from jax.experimental import pallas as pl
from jax.experimental.pallas import tpu as pltpu
from jax.sharding import PartitionSpec as P

MESH = pl.DeviceIdType.MESH
F32 = jnp.float32
BF16 = jnp.bfloat16

NS = 8
NT = 8
NG = 16
HALF = 4
LN2 = math.log(2.0)
SCALE = 5.0 / LN2**2
SHIFT = 1.5 / LN2
CONST = 0.75 / LN2**2
FACTOR = LN2**2 / 3.0 * 2.0**SHIFT
WIDTH = 256


def entries(x, factor=None):
    t = jnp.maximum(x, 1e-12)
    w = -SHIFT - t * lax.rsqrt(t)
    value = (w * w + CONST) * jnp.exp2(w)
    return (value if factor is None else value * factor).astype(BF16)


def pieces(value):
    high = value.astype(BF16).astype(F32)
    mid = (value - high).astype(BF16).astype(F32)
    low = (value - high - mid).astype(BF16).astype(F32)
    return high, mid, low


def kernel(
    coords_hbm, scale_hbm, residual_hbm, direction_hbm, image_ref, coef_ref,
    coords, scale, residual, direction,
    blk, left, right, dir_s, acc_s, acc_t, out, got, x0, x1, k0, k1, mine, part, one, two,
    load, blk_send, blk_recv, out_send, out_recv, one_send, one_recv, two_send, two_recv,
):
    row, col = lax.axis_index("row"), lax.axis_index("col")
    core, y = row % 2, (row // 2) % 4
    z = (col // 4) * 2 + row // 8
    group = ((z + 2 * y) % 4) * 4 + y
    member = (col % 4) * 2 + core

    def device(dg, dm):
        g, m = (group + dg + NG) % NG, (member + dm + NS) % NS
        y = g % 4
        z = (2 * y + g // 4) % 4
        return ((z % 2) * 8 + y * 2 + m % 2, (z // 2) * 4 + m // 2)

    loads = [
        pltpu.make_async_copy(src, dst, load.at[i])
        for i, (src, dst) in enumerate(
            ((coords_hbm, coords), (scale_hbm, scale), (direction_hbm, direction), (residual_hbm, residual))
        )
    ]
    for copy in loads:
        copy.start()

    barrier = pltpu.get_barrier_semaphore()
    for s in range(1, NS):
        pl.semaphore_signal(barrier, inc=1, device_id=device(0, s), device_id_type=MESH)
    for t in range(1, NG):
        pl.semaphore_signal(barrier, inc=1, device_id=device(t, 0), device_id_type=MESH)

    def remote(src, dst, send, recv, dg, dm):
        return pltpu.make_async_remote_copy(
            src_ref=src, dst_ref=dst, send_sem=send, recv_sem=recv, device_id=device(dg, dm), device_id_type=MESH
        )

    def s_copy(s):
        return remote(blk.at[0], blk.at[s], blk_send.at[s], blk_recv.at[s], 0, s)

    def t_copy(t):
        slot = NS - 1 + t
        return remote(blk.at[0], blk.at[slot], blk_send.at[slot], blk_recv.at[slot], -t, 0)

    def out_copy(slot, dg, dm):
        return remote(out.at[slot], got.at[slot], out_send.at[slot], out_recv.at[slot], dg, dm)

    for copy in loads[0:3]:
        copy.wait()
    eye = lax.broadcasted_iota(jnp.int32, (16, 16), 0) == lax.broadcasted_iota(jnp.int32, (16, 16), 1)
    column = jnp.sum(jnp.where(eye, jnp.broadcast_to(scale[...], (16, 16)), 0.0), axis=1, keepdims=True)
    blk[0, 0:16, :] = (coords[...] / column).astype(BF16)
    blk[0, 16:80, :] = direction[...].astype(BF16)

    pl.semaphore_wait(barrier, NS - 1 + NG - 1)
    for s in range(1, HALF):
        s_copy(s).start()
    for t in (4, 5, 6):
        t_copy(t).start()
    for s in range(HALF, NS):
        s_copy(s).start()
    for t in (7, 1, 2, 3, 8):
        t_copy(t).start()

    def features(slot):
        wide = blk[slot, 0:16, :].astype(F32)
        high, mid, low = pieces(jnp.sum(wide * wide, axis=0, keepdims=True))
        rows = lax.broadcasted_iota(jnp.int32, (8, 512), 0)
        norm = jnp.where(rows == 0, high, jnp.where(rows == 1, mid, jnp.where(rows == 2, low, 0.0)))
        return wide, norm, jnp.where(rows < 3, 1.0, 0.0)

    def prepare_s(s):
        wide, norm, ones = features(s)
        turned = jnp.concatenate([wide * (-2.0 * SCALE), ones * SCALE, norm * SCALE], axis=0)
        high, mid, low = pieces(turned)
        right[s, 0:32, :] = high.astype(BF16)
        right[s, 32:64, :] = mid.astype(BF16)
        right[s, 64:96, :] = low.astype(BF16)
        dir_s[s] = blk[s, 16:80, :]

    def prepare_t(slot):
        wide, norm, ones = features(slot)
        one_set = jnp.concatenate([wide, norm, ones], axis=0)
        four = jnp.concatenate([one_set, one_set, one_set, jnp.zeros_like(one_set)], axis=0)
        left[...] = four.T.astype(BF16)

    def cross(x, s, half):
        for j in range(0, 512, WIDTH):
            x[j : j + WIDTH, :] = lax.dot_general(
                left[j : j + WIDTH, 0:96], right[s, :, half * WIDTH : (half + 1) * WIDTH],
                (((1,), (0,)), ((), ())), preferred_element_type=F32,
            )

    def fill(k, x, factor=None):
        for j in range(0, 512, WIDTH):
            k[j : j + WIDTH, :] = entries(x[j : j + WIDTH, :], factor)

    def add_s(k, s, half, slot):
        cols = slice(half * WIDTH, (half + 1) * WIDTH)
        acc_s[s, :, cols] += lax.dot_general(
            blk[slot, 16:80, :], k[...], (((1,), (0,)), ((), ())), preferred_element_type=F32
        )

    def add_t(k, s, half):
        cols = slice(half * WIDTH, (half + 1) * WIDTH)
        acc_t[...] += lax.dot_general(
            dir_s[s, :, cols], k[...], (((1,), (1,)), ((), ())), preferred_element_type=F32
        )

    xs, ks = (x0, x1), (k0, k1)

    def strip(base, sides, slot):
        prepare_t(slot)
        acc_t[...] = jnp.zeros_like(acc_t)
        groups = 2 * len(sides)
        for g in range(groups + 2):
            if g < groups:
                cross(xs[g % 2], base + g // 2, g % 2)
            if g >= 2:
                add_s(ks[g % 2], base + (g - 2) // 2, g % 2, slot)
                if sides[(g - 2) // 2]:
                    add_t(ks[g % 2], base + (g - 2) // 2, g % 2)
            if 1 <= g <= groups:
                fill(ks[(g - 1) % 2], xs[(g - 1) % 2])

    acc_s[...] = jnp.zeros_like(acc_s)
    prepare_s(0)
    prepare_t(0)
    for half in range(2):
        cross(xs[half], 0, half)
        fill(ks[half], xs[half], FACTOR)
        add_s(ks[half], 0, half, 0)
    acc_s[0] = acc_s[0] * (1.0 / FACTOR)

    def first(i, carry):
        t = (i + 3) % 7 + 1
        t_copy(t).wait_recv()
        strip(0, (True,) * HALF, NS - 1 + t)
        part[t - 1] = acc_t[...]
        return carry

    def middle(u, carry):
        strip(1, (True, True, True, False), u * 15)

        @pl.when(u == 0)
        def _():
            acc_s[0] += acc_t[...]

        return carry

    def second(i, carry):
        t = (i + 4) % 7 + 1
        strip(HALF, (True,) * HALF, NS - 1 + t)
        out[NS - 2 + t] = (acc_t[...] + part[t - 1]).astype(BF16)
        out_copy(NS - 2 + t, t, 0).start()
        return carry

    def send_s(s):
        out[s - 1] = acc_s[s].astype(BF16)
        out_copy(s - 1, 0, -s).start()

    for s in range(1, HALF):
        s_copy(s).wait_recv()
        prepare_s(s)
    lax.fori_loop(0, 7, first, 0)
    for s in range(HALF, NS):
        s_copy(s).wait_recv()
        prepare_s(s)
    t_copy(8).wait_recv()
    lax.fori_loop(0, 2, middle, 0)
    out[14] = acc_t[...].astype(BF16)
    out_copy(14, 8, 0).start()
    for s in range(1, HALF):
        send_s(s)
    lax.fori_loop(0, 7, second, 0)
    for s in range(HALF, NS):
        send_s(s)
    prepare_t(15)
    for half in range(2):
        cross(xs[half], 0, half)
        fill(ks[half], xs[half])
        add_s(ks[half], 0, half, 15)

    loads[3].wait()
    res, dirn = residual[...], direction[...]
    total = acc_s[0]
    for slot in (0, 1, 2, 14, 11, 12, 13, 7, 8, 9, 10, 3, 4, 5, 6):
        out_copy(slot, 0, 0).wait_recv()
        total = total + got[slot].astype(F32)
    image = total * FACTOR + dirn
    image_ref[...] = image

    def lanes(value):
        return jnp.sum(value, axis=1, keepdims=True)

    lane = lax.broadcasted_iota(jnp.int32, (64, 128), 1)
    table = jnp.where(lane == 0, lanes(res * res), 0.0)
    table = jnp.where(lane == 1, lanes(dirn * image), table)
    table = jnp.where(lane == 2, lanes(res * image), table)
    table = jnp.where(lane == 3, lanes(image * image), table)
    mine[...] = jnp.concatenate([table, jnp.zeros_like(table)], axis=0).T[0:8, :]

    def one_copy(s):
        return remote(mine, one.at[s], one_send.at[s], one_recv.at[s], 0, s)

    def two_copy(t):
        return remote(two.at[0], two.at[t], two_send.at[t], two_recv.at[t], t, 0)

    for s in range(1, NS):
        one_copy(s).start()
    value = mine[...]
    for s in range(1, NS):
        one_copy(s).wait_recv()
        value = value + one[s]
    two[0] = value
    for t in range(1, NG):
        two_copy(t).start()
    for t in range(1, NG):
        two_copy(t).wait_recv()
        value = value + two[t]

    square = jnp.concatenate([value, jnp.zeros((120, 128), F32)], axis=0).T
    norm_old, curv = square[0:64, 0:1], square[0:64, 1:2]
    mixed, norm_image = square[0:64, 2:3], square[0:64, 3:4]
    alpha = norm_old / curv
    fresh = jnp.maximum(norm_old - alpha * (2.0 * mixed - alpha * norm_image), 0.0)
    beta = fresh / norm_old
    coef_ref[...] = jnp.where(lane == 0, alpha, jnp.where(lane == 1, beta, 0.0))

    for s in range(1, NS):
        s_copy(s).wait_send()
        one_copy(s).wait_send()
    for t in range(1, NT + 1):
        t_copy(t).wait_send()
    for slot in range(15):
        out_copy(slot, 0, 0).wait_send()
    for t in range(1, NG):
        two_copy(t).wait_send()


def local(coords, lengthscale, solution, residual, direction):
    probes, points = direction.shape
    feats = coords.shape[0]
    dma = pltpu.SemaphoreType.DMA
    image, coef = pl.pallas_call(
        kernel,
        out_shape=(jax.ShapeDtypeStruct((probes, points), F32), jax.ShapeDtypeStruct((probes, 128), F32)),
        in_specs=[pl.BlockSpec(memory_space=pl.ANY)] * 4,
        out_specs=[pl.BlockSpec(memory_space=pltpu.VMEM)] * 2,
        scratch_shapes=[
            pltpu.VMEM((feats, points), F32),
            pltpu.VMEM((1, feats), F32),
            pltpu.VMEM((probes, points), F32),
            pltpu.VMEM((probes, points), F32),
            pltpu.VMEM((16, 80, 512), BF16),
            pltpu.VMEM((512, 128), BF16),
            pltpu.VMEM((NS, 96, 512), BF16),
            pltpu.VMEM((NS, 64, 512), BF16),
            pltpu.VMEM((NS, 64, 512), F32),
            pltpu.VMEM((64, 512), F32),
            pltpu.VMEM((15, 64, 512), BF16),
            pltpu.VMEM((15, 64, 512), BF16),
            pltpu.VMEM((512, WIDTH), F32),
            pltpu.VMEM((512, WIDTH), F32),
            pltpu.VMEM((512, WIDTH), BF16),
            pltpu.VMEM((512, WIDTH), BF16),
            pltpu.VMEM((8, 128), F32),
            pltpu.VMEM((NT, 64, 512), F32),
            pltpu.VMEM((NS, 8, 128), F32),
            pltpu.VMEM((NG, 8, 128), F32),
            dma((4,)), dma((16,)), dma((16,)), dma((15,)), dma((15,)), dma((8,)), dma((8,)), dma((16,)), dma((16,)),
        ],
        compiler_params=pltpu.CompilerParams(
            collective_id=0, has_side_effects=True, vmem_limit_bytes=48 * 2**20
        ),
    )(coords, lengthscale[None, :], residual, direction)
    alpha, beta = coef[:, 0:1], coef[:, 1:2]
    new_residual = residual - alpha * image
    return solution + alpha * direction, new_residual, new_residual + beta * direction


def solution(mesh):
    spec = P(None, ("row", "col"))
    return jax.shard_map(
        local, mesh=mesh, in_specs=(spec, P(), spec, spec, spec), out_specs=(spec, spec, spec), check_vma=False
    )
```

time: 82.2 us -> 68.5 us (0.83)
  Pallas kernels: 75.1 us -> 63.4 us
  local copies, waits for them, and re-layouts: 6.17 us -> 3.39 us
  other arithmetic: 0 us -> 0.84 us
    pallas_call x1, Pallas kernels: 75.1 us -> 63.4 us  [local(): pl.pallas_call(kernel, out_shape=(jax.ShapeDtypeStruct((probes, points),...]
    unnamed x13 -> x10, local copies, waits for them, and re-layouts: 6.08 us -> 3.22 us
    add x0 -> x1, other arithmetic: none -> 0.84 us  [local(): new_residual + beta * direction]
where the time goes in v2:
time: 68.5 us; the launch traced here: 68.3 us
  Pallas kernels  63.4 us (93%)
  local copies, waits for them, and re-layouts  3.39 us (5%)
  other arithmetic  0.84 us (1%)
    pallas_call x1, Pallas kernels, local(): pl.pallas_call(kernel, out_shape=(jax.ShapeDtypeStruct((probes, points),...  63.4 us
    unnamed x10, local copies, waits for them, and re-layouts  3.22 us

profile of v2, /device:TPU:1, one launch (start us, length us, event | category | flops | bytes accessed | tf_op | source)
XLA Modules:
  0.0 68.3 jit_solution(2724694164662967718)
XLA Ops:
  0.6 0.0 copy-start.3
  0.6 0.6 copy-done.3
  1.3 0.0 copy-start
  1.3 0.9 %copy-done = f32[64,512]{1,0:T(8,128)S(1)} copy-done((f32[64,512]{1,0:T(8,128)S(1)}, f32[64,512]{1,0:T(8,128)}, u32[]{:S(2)}) %copy-start) | copy-done | bytes 131096
  2.2 0.0 copy-start.1
  2.2 0.9 %copy-done.1 = f32[64,512]{1,0:T(8,128)S(1)} copy-done((f32[64,512]{1,0:T(8,128)S(1)}, f32[64,512]{1,0:T(8,128)}, u32[]{:S(2)}) %copy-start.1) | copy-done | bytes 131096
  3.1 0.0 copy-start.2
  3.1 0.8 %copy-done.2 = f32[16,512]{1,0:T(8,128)S(1)} copy-done((f32[16,512]{1,0:T(8,128)S(1)}, f32[16,512]{1,0:T(8,128)}, u32[]{:S(2)}) %copy-start.2) | copy-done | bytes 32792
  3.9 0.0 copy-start.4
  3.9 63.4 %shard_map.76 = (f32[64,512]{1,0:T(8,128)S(1)}, f32[64,128]{1,0:T(8,128)S(1)}) custom-call(f32[16,512]{1,0:T(8,128)S(1)} %copy-done.2, f32[1,16]{1,0:T(1,128)S(1)} %bitcast.1, f32[64,512]{1,0:T(8,128)S(1)} %copy-done.1, f32[64,512]{1,0:T(8,128)S(1)} %copy-done), custom_call_target="tpu_custom_call" | custom-call | tf_op jit(solution)/shard_map/pallas_call | solution.py:285
  67.2 0.2 slice_reduce_fusion
  67.4 0.0 copy-done.4
  67.4 0.8 %multiply_add_fusion = (f32[64,512]{1,0:T(8,128)}, f32[64,512]{1,0:T(8,128)}, f32[64,512]{1,0:T(8,128)}) fusion(f32[64,512]{1,0:T(8,128)S(1)} %copy-done, f32[64]{0:T(128)S(1)} %get-tuple-element.7, f32[64,512]{1,0:T(8,128)S(1)} %copy-done.1, f32[64,512]{1,0:T(8,128)S(1)} %get-tuple-element.6, f32[64]{0:T(128)S(1)} %get-tuple-element.8, f32[64,512]{1,0:T(8,128)S(1)} %copy-done.4), kind=kLoop, calls=%fused_computation | loop fusion | flops 196608 | bytes 918016 | tf_op jit(solution)/shard_map/add | solution.py:319
Async XLA Ops:
  0.6 0.7 copy-start.3
  1.3 0.9 %copy-start = (f32[64,512]{1,0:T(8,128)S(1)}, f32[64,512]{1,0:T(8,128)}, u32[]{:S(2)}) copy-start(f32[64,512]{1,0:T(8,128)} %direction_hbm.1) | copy-start | bytes 393220
  2.2 0.9 %copy-start.1 = (f32[64,512]{1,0:T(8,128)S(1)}, f32[64,512]{1,0:T(8,128)}, u32[]{:S(2)}) copy-start(f32[64,512]{1,0:T(8,128)} %residual_hbm.1) | copy-start | bytes 393220
  3.1 0.8 %copy-start.2 = (f32[16,512]{1,0:T(8,128)S(1)}, f32[16,512]{1,0:T(8,128)}, u32[]{:S(2)}) copy-start(f32[16,512]{1,0:T(8,128)} %coords_hbm.1) | copy-start | bytes 98308
  3.9 63.5 %copy-start.4 = (f32[64,512]{1,0:T(8,128)S(1)}, f32[64,512]{1,0:T(8,128)}, u32[]{:S(2)}) copy-start(f32[64,512]{1,0:T(8,128)} %param.7) | copy-start | bytes 393220

commit v3 on v2

v3 whole, which is shorter than its diff:
```python
import math

import jax
import jax.numpy as jnp
from jax import lax
from jax.experimental import pallas as pl
from jax.experimental.pallas import tpu as pltpu
from jax.sharding import PartitionSpec as P

MESH = pl.DeviceIdType.MESH
F32 = jnp.float32
BF16 = jnp.bfloat16

NS = 8
NT = 8
NG = 16
HALF = 4
LN2 = math.log(2.0)
SCALE = 5.0 / LN2**2
SHIFT = 1.5 / LN2
CONST = 0.75 / LN2**2
FACTOR = LN2**2 / 3.0 * 2.0**SHIFT
WIDTH = 256
VMEM = 60 * 2**20


def entries(x, factor=None):
    t = jnp.maximum(x, 1e-12)
    w = -SHIFT - t * lax.rsqrt(t)
    value = (w * w + CONST) * jnp.exp2(w)
    return (value if factor is None else value * factor).astype(BF16)


def pieces(value):
    high = value.astype(BF16).astype(F32)
    mid = (value - high).astype(BF16).astype(F32)
    low = (value - high - mid).astype(BF16).astype(F32)
    return high, mid, low


def kernel(
    coords_hbm, scale_hbm, residual_hbm, direction_hbm, image_ref, coef_ref,
    coords, scale, residual, direction,
    blk, left, right, dir_s, acc, out, got, x0, x1, k0, k1, mine, one, two,
    load, blk_send, blk_recv, out_send, out_recv, one_send, one_recv, two_send, two_recv,
):
    row, col = lax.axis_index("row"), lax.axis_index("col")
    core, y, z_lo = lax.rem(row, 2), lax.rem(lax.div(row, 2), 4), lax.div(row, 8)
    x, z_hi = lax.rem(col, 4), lax.div(col, 4)
    group = lax.rem(z_hi * 2 + z_lo + 2 * y, 4) * 4 + y
    member = core * 4 + x

    ring = {}
    for s in range(1, NS):
        m = lax.rem(member + s, NS)
        ring[s] = (row - core + lax.div(m, 4), z_hi * 4 + lax.rem(m, 4))

    def across(t):
        g = lax.rem(group + t, NG)
        to_y = lax.rem(g, 4)
        to_z = lax.rem(2 * to_y + lax.div(g, 4), 4)
        return (lax.rem(to_z, 2) * 8 + to_y * 2 + core, lax.div(to_z, 2) * 4 + x)

    plane = {t: across(t) for t in range(1, NG)}

    loads = [
        pltpu.make_async_copy(src, dst, load.at[i])
        for i, (src, dst) in enumerate(
            ((coords_hbm, coords), (scale_hbm, scale), (direction_hbm, direction), (residual_hbm, residual))
        )
    ]
    for copy in loads:
        copy.start()

    barrier = pltpu.get_barrier_semaphore()
    for s in range(1, NS):
        pl.semaphore_signal(barrier, inc=1, device_id=ring[s], device_id_type=MESH)
    for t in range(1, NG):
        pl.semaphore_signal(barrier, inc=1, device_id=plane[t], device_id_type=MESH)

    def remote(src, dst, send, recv, where):
        return pltpu.make_async_remote_copy(
            src_ref=src, dst_ref=dst, send_sem=send, recv_sem=recv, device_id=where, device_id_type=MESH
        )

    def s_copy(s):
        return remote(blk.at[0], blk.at[s], blk_send.at[s], blk_recv.at[s], ring[s])

    def t_copy(t, where=None):
        slot = NS + t
        return remote(blk.at[0], blk.at[slot], blk_send.at[slot], blk_recv.at[slot], where or ring[1])

    def out_copy(slot, where=None):
        return remote(out.at[slot], got.at[slot], out_send.at[slot], out_recv.at[slot], where or ring[1])

    for copy in loads[0:3]:
        copy.wait()
    eye = lax.broadcasted_iota(jnp.int32, (16, 16), 0) == lax.broadcasted_iota(jnp.int32, (16, 16), 1)
    column = jnp.sum(jnp.where(eye, jnp.broadcast_to(scale[...], (16, 16)), 0.0), axis=1, keepdims=True)
    blk[0, 0:16, :] = (coords[...] / column).astype(BF16)
    blk[0, 16:80, :] = direction[...].astype(BF16)
    blk[NS] = blk[0]

    def features(slot):
        wide = blk[slot, 0:16, :].astype(F32)
        high, mid, low = pieces(jnp.sum(wide * wide, axis=0, keepdims=True))
        rows = lax.broadcasted_iota(jnp.int32, (8, 512), 0)
        norm = jnp.where(rows == 0, high, jnp.where(rows == 1, mid, jnp.where(rows == 2, low, 0.0)))
        return wide, norm, jnp.where(rows < 3, 1.0, 0.0)

    def prepare_s(s):
        wide, norm, ones = features(s)
        one_set = jnp.concatenate([wide, norm, ones], axis=0)
        four = jnp.concatenate([one_set, one_set, one_set, jnp.zeros_like(one_set)], axis=0)
        left[s] = four.T.astype(BF16)
        dir_s[s] = blk[s, 16:80, :]

    def prepare_t(t):
        wide, norm, ones = features(NS + t)
        turned = jnp.concatenate([wide * (-2.0 * SCALE), ones * SCALE, norm * SCALE], axis=0)
        high, mid, low = pieces(turned)
        right[t, 0:32, :] = high.astype(BF16)
        right[t, 32:64, :] = mid.astype(BF16)
        right[t, 64:96, :] = low.astype(BF16)

    def cross(x, s, t, half):
        for j in range(0, 512, WIDTH):
            x[j : j + WIDTH, :] = lax.dot_general(
                left[s, j : j + WIDTH, 0:96], right[t, :, half * WIDTH : (half + 1) * WIDTH],
                (((1,), (0,)), ((), ())), preferred_element_type=F32,
            )

    def fill(k, x, half, factor=None):
        for j in range(0, 512, WIDTH):
            k[j : j + WIDTH, half * WIDTH : (half + 1) * WIDTH] = entries(x[j : j + WIDTH, :], factor)

    def to_t(k, s, t):
        acc[NS + t] += lax.dot_general(dir_s[s], k[...], (((1,), (0,)), ((), ())), preferred_element_type=F32)

    def to_s(k, s, t):
        acc[s] += lax.dot_general(
            blk[NS + t, 16:80, :], k[...], (((1,), (1,)), ((), ())), preferred_element_type=F32
        )

    acc[...] = jnp.zeros_like(acc)
    k1[...] = jnp.zeros_like(k1)
    dir_s[NS] = jnp.zeros_like(dir_s[NS])
    prepare_s(0)
    prepare_t(0)
    cross(x0, 0, 0, 0)
    cross(x1, 0, 0, 1)
    fill(k0, x0, 0, FACTOR)
    fill(k0, x1, 1, FACTOR)
    to_s(k0, 0, 0)
    acc[0] = acc[0] * (1.0 / FACTOR)

    pl.semaphore_wait(barrier, NS - 1 + NG - 1)
    for s in (4, 1, 3, 2):
        s_copy(s).start()
    for t in (4, 5, 6):
        t_copy(t, plane[NG - t]).start()


    def plan(q):
        late = q > 8
        t = jnp.where(late, lax.rem(lax.max(q - 9, 0) + 4, 7) + 1, lax.rem(q + 2, 7) + 1)
        t = jnp.where(q == 8, 8, t)
        base = jnp.where(q == 8, 1, jnp.where(late, HALF, 0))
        slots = [base, base + 1, base + 2, base + 3]
        return t, slots, slots[0:3] + [jnp.where(q == 8, NS, base + 3)]

    ks = (k0, k1)

    def slot_step(i, now, old, following):
        (s, t), (old_s, old_dir, old_t) = now, old
        cross(x1, s, t, 1)
        to_t(ks[1 - i % 2], old_dir, old_t)
        fill(ks[i % 2], x0, 0)
        if following is not None:
            cross(x0, following[0], following[1], 0)
        to_s(ks[1 - i % 2], old_s, old_t)
        fill(ks[i % 2], x1, 1)

    def strip(q, carry):
        t, slots, dirs = plan(q)
        before_t, before_slots, before_dirs = plan(q - 1)
        before_t = jnp.where(q == 1, 0, before_t)
        before_slots = before_slots[0:3] + [jnp.where(q == 1, 2, before_slots[3])]
        before_dirs = before_dirs[0:3] + [jnp.where(q == 1, 2, before_dirs[3])]
        after_t, after_slots, _ = plan(q + 1)
        after_slots = [jnp.where(q == 13, 5, after_slots[0])]

        @pl.when(q < 7)
        def _():
            t_copy(after_t).wait_recv()
            prepare_t(after_t)

        @pl.when(q < 4)
        def _():
            later = lax.rem(q + 6, 7) + 1
            t_copy(later, across(NG - later)).start()

        @pl.when(q == 1)
        def _():
            for s in (5, 7, 6):
                s_copy(s).start()

        @pl.when(q == 4)
        def _():
            t_copy(8, plane[8]).start()

        @pl.when(q == 7)
        def _():
            t_copy(8).wait_recv()
            prepare_t(8)
            for s in range(HALF + 1, NS):
                s_copy(s).wait_recv()
                prepare_s(s)

        old = (before_slots[3], before_dirs[3], before_t)
        for i in range(4):
            following = (after_slots[0], after_t) if i == 3 else (slots[i + 1], t)
            slot_step(i, (slots[i], t), old, following)
            old = (slots[i], dirs[i], t)

        @pl.when(q == 9)
        def _():
            send_t(8, plane[8])
            for s in range(1, HALF):
                send_s(s)

        @pl.when(q > 9)
        def _():
            send_t(before_t, across(before_t))

        return carry

    def send_t(t, where):
        out[NS - 2 + t] = acc[NS + t].astype(BF16)
        out_copy(NS - 2 + t, where).start()

    def send_s(s):
        out[s - 1] = acc[s].astype(BF16)
        out_copy(s - 1, ring[NS - s]).start()

    old = (1, NS, 0)
    order = (4, 1, 3, 2)
    for i, s in enumerate(order):
        if i == 0:
            s_copy(s).wait_recv()
            prepare_s(s)
            cross(x0, s, 0, 0)
        if i < 3:
            s_copy(order[i + 1]).wait_recv()
            prepare_s(order[i + 1])
            following = (order[i + 1], 0)
        else:
            t_copy(4).wait_recv()
            prepare_t(4)
            following = (0, 4)
        slot_step(i, (s, 0), old, following)
        old = (s, NS if s == HALF else s, 0)
    t_copy(7, plane[NG - 7]).start()
    lax.fori_loop(1, 14, strip, 0)
    order = [(s, t) for s in (5, 6, 7, 4) for t in (3, 4)]
    old = (7, 7, 2)
    for i, (s, t) in enumerate(order):
        slot_step(i, (s, t), old, order[i + 1] if i < 7 else None)
        if i == 0:
            send_t(2, plane[2])
        elif i % 2 == 0:
            send_s(order[i - 1][0])
        old = (s, s, t)
    send_t(3, plane[3])
    to_t(k1, 4, 4)
    send_t(4, plane[4])
    to_s(k1, 4, 4)
    send_s(4)
    cross(x0, 0, 8, 0)
    cross(x1, 0, 8, 1)
    fill(k0, x0, 0)
    fill(k0, x1, 1)
    to_s(k0, 0, 8)

    loads[3].wait()
    res, dirn = residual[...], direction[...]
    total = acc[0] + acc[NS]
    for slot in (0, 1, 2, 14, 11, 12, 13, 7, 8, 4, 5, 6, 9, 3, 10):
        out_copy(slot).wait_recv()
        total = total + got[slot].astype(F32)
    image = total * FACTOR + dirn
    image_ref[...] = image

    def lanes(value):
        return jnp.sum(value, axis=1, keepdims=True)

    lane = lax.broadcasted_iota(jnp.int32, (64, 128), 1)
    table = jnp.where(lane == 0, lanes(res * res), 0.0)
    table = jnp.where(lane == 1, lanes(dirn * image), table)
    table = jnp.where(lane == 2, lanes(res * image), table)
    table = jnp.where(lane == 3, lanes(image * image), table)
    mine[...] = jnp.concatenate([table, jnp.zeros_like(table)], axis=0).T[0:8, :]

    def one_copy(s):
        return remote(mine, one.at[s], one_send.at[s], one_recv.at[s], ring[s])

    def two_copy(t):
        return remote(two.at[0], two.at[t], two_send.at[t], two_recv.at[t], plane[t])

    for s in range(1, NS):
        one_copy(s).start()
    value = mine[...]
    for s in range(1, NS):
        one_copy(s).wait_recv()
        value = value + one[s]
    two[0] = value
    for t in range(1, NG):
        two_copy(t).start()
    for t in range(1, NG):
        two_copy(t).wait_recv()
        value = value + two[t]

    square = jnp.concatenate([value, jnp.zeros((120, 128), F32)], axis=0).T
    norm_old, curv = square[0:64, 0:1], square[0:64, 1:2]
    mixed, norm_image = square[0:64, 2:3], square[0:64, 3:4]
    alpha = norm_old / curv
    fresh = jnp.maximum(norm_old - alpha * (2.0 * mixed - alpha * norm_image), 0.0)
    beta = fresh / norm_old
    coef_ref[...] = jnp.where(lane == 0, alpha, jnp.where(lane == 1, beta, 0.0))

    for s in range(1, NS):
        s_copy(s).wait_send()
        one_copy(s).wait_send()
    for t in range(1, NT + 1):
        t_copy(t).wait_send()
    for slot in range(15):
        out_copy(slot).wait_send()
    for t in range(1, NG):
        two_copy(t).wait_send()


def local(coords, lengthscale, solution, residual, direction):
    probes, points = direction.shape
    feats = coords.shape[0]
    dma = pltpu.SemaphoreType.DMA
    image, coef = pl.pallas_call(
        kernel,
        out_shape=(jax.ShapeDtypeStruct((probes, points), F32), jax.ShapeDtypeStruct((probes, 128), F32)),
        in_specs=[pl.BlockSpec(memory_space=pl.ANY)] * 4,
        out_specs=[pl.BlockSpec(memory_space=pltpu.VMEM)] * 2,
        scratch_shapes=[
            pltpu.VMEM((feats, points), F32),
            pltpu.VMEM((1, feats), F32),
            pltpu.VMEM((probes, points), F32),
            pltpu.VMEM((probes, points), F32),
            pltpu.VMEM((17, 80, 512), BF16),
            pltpu.VMEM((NS, 512, 128), BF16),
            pltpu.VMEM((NT + 1, 96, 512), BF16),
            pltpu.VMEM((NS + 1, 64, 512), BF16),
            pltpu.VMEM((17, 64, 512), F32),
            pltpu.VMEM((15, 64, 512), BF16),
            pltpu.VMEM((15, 64, 512), BF16),
            pltpu.VMEM((512, WIDTH), F32),
            pltpu.VMEM((512, WIDTH), F32),
            pltpu.VMEM((512, 512), BF16),
            pltpu.VMEM((512, 512), BF16),
            pltpu.VMEM((8, 128), F32),
            pltpu.VMEM((NS, 8, 128), F32),
            pltpu.VMEM((NG, 8, 128), F32),
            dma((4,)), dma((17,)), dma((17,)), dma((15,)), dma((15,)), dma((8,)), dma((8,)), dma((16,)), dma((16,)),
        ],
        compiler_params=pltpu.CompilerParams(
            collective_id=0, has_side_effects=True, vmem_limit_bytes=VMEM
        ),
    )(coords, lengthscale[None, :], residual, direction)
    alpha, beta = coef[:, 0:1], coef[:, 1:2]
    new_residual = residual - alpha * image
    return solution + alpha * direction, new_residual, new_residual + beta * direction


def solution(mesh):
    spec = P(None, ("row", "col"))
    return jax.shard_map(
        local, mesh=mesh, in_specs=(spec, P(), spec, spec, spec), out_specs=(spec, spec, spec), check_vma=False
    )
```

time: 68.5 us -> 65.8 us (0.961)
  local copies, waits for them, and re-layouts: 3.39 us -> 1.02 us
  Pallas kernels: 63.4 us -> 61.9 us
  other arithmetic: 0.84 us -> 1.81 us
    unnamed x10 -> x4, local copies, waits for them, and re-layouts: 3.22 us -> 0.01 us
    pallas_call x1, Pallas kernels: 63.4 us -> 61.9 us  [local(): pl.pallas_call(kernel, out_shape=(jax.ShapeDtypeStruct((probes, points),...]
    add x1, other arithmetic: 0.84 us -> 1.81 us  [local(): new_residual + beta * direction]
    slice x1, local copies, waits for them, and re-layouts: 0.17 us -> 1.01 us  [local(): alpha, beta = (coef[:, 0:1], coef[:, 1:2])]
where the time goes in v3:
time: 65.8 us; the launch traced here: 65.4 us
  Pallas kernels  61.9 us (94%)
  other arithmetic  1.81 us (3%)
  local copies, waits for them, and re-layouts  1.02 us (2%)
  between operations  0.68 us (1%)
    pallas_call x1, Pallas kernels, local(): pl.pallas_call(kernel, out_shape=(jax.ShapeDtypeStruct((probes, points),...  61.9 us
    add x1, other arithmetic, local(): new_residual + beta * direction  1.81 us

profile of v3, /device:TPU:1, one launch (start us, length us, event | category | flops | bytes accessed | tf_op | source)
XLA Modules:
  0.0 65.4 jit_solution(12346310215859165655)
XLA Ops:
  0.6 0.0 copy-start
  0.6 0.0 copy-start.1
  0.7 61.9 %shard_map.76 = (f32[64,512]{1,0:T(8,128)}, f32[64,128]{1,0:T(8,128)}) custom-call(f32[16,512]{1,0:T(8,128)} %coords_hbm.1, f32[1,16]{1,0:T(1,128)} %bitcast.1, f32[64,512]{1,0:T(8,128)} %residual_hbm.1, f32[64,512]{1,0:T(8,128)} %direction_hbm.1), custom_call_target="tpu_custom_call" | custom-call | tf_op jit(solution)/shard_map/pallas_call | solution.py:346
  62.5 1.0 %slice_reduce_fusion = (f32[64]{0:T(128)S(1)}, f32[64]{0:T(128)S(1)}) fusion(f32[64,128]{1,0:T(8,128)} %get-tuple-element.5), kind=kLoop, calls=%fused_computation.3 | loop fusion | bytes 1024 | tf_op jit(solution)/shard_map/slice | solution.py:376
  63.5 0.0 copy-done
  63.6 0.0 copy-done.1
  63.6 1.8 %multiply_add_fusion = (f32[64,512]{1,0:T(8,128)}, f32[64,512]{1,0:T(8,128)}, f32[64,512]{1,0:T(8,128)}) fusion(f32[64,512]{1,0:T(8,128)S(1)} %copy-done, f32[64]{0:T(128)S(1)} %get-tuple-element.7, f32[64,512]{1,0:T(8,128)S(1)} %copy-done.1, f32[64,512]{1,0:T(8,128)} %get-tuple-element.6, f32[64]{0:T(128)S(1)} %get-tuple-element.8, f32[64,512]{1,0:T(8,128)} %param.7), kind=kLoop, calls=%fused_computation | loop fusion | flops 196608 | bytes 918016 | tf_op jit(solution)/shard_map/add | solution.py:378
Async XLA Ops:
  0.6 62.9 %copy-start = (f32[64,512]{1,0:T(8,128)S(1)}, f32[64,512]{1,0:T(8,128)}, u32[]{:S(2)}) copy-start(f32[64,512]{1,0:T(8,128)} %direction_hbm.1) | copy-start | bytes 393220
  0.6 62.9 %copy-start.1 = (f32[64,512]{1,0:T(8,128)S(1)}, f32[64,512]{1,0:T(8,128)}, u32[]{:S(2)}) copy-start(f32[64,512]{1,0:T(8,128)} %residual_hbm.1) | copy-start | bytes 393220

commit v4 on v3

--- a/solution.py
+++ b/solution.py
@@ -25,8 +25,7 @@
 
 
 def entries(x, factor=None):
-    t = jnp.maximum(x, 1e-12)
-    w = -SHIFT - t * lax.rsqrt(t)
+    w = -SHIFT - x * lax.rsqrt(x)
     value = (w * w + CONST) * jnp.exp2(w)
     return (value if factor is None else value * factor).astype(BF16)
 
@@ -39,7 +38,7 @@
 
 
 def kernel(
-    coords_hbm, scale_hbm, residual_hbm, direction_hbm, image_ref, coef_ref,
+    coords_hbm, scale_hbm, residual_hbm, direction_hbm, image_ref, alpha_ref, beta_ref,
     coords, scale, residual, direction,
     blk, left, right, dir_s, acc, out, got, x0, x1, k0, k1, mine, one, two,
     load, blk_send, blk_recv, out_send, out_recv, one_send, one_recv, two_send, two_recv,
@@ -125,61 +124,65 @@
 
     def cross(x, s, t, half):
         for j in range(0, 512, WIDTH):
-            x[j : j + WIDTH, :] = lax.dot_general(
+            dist = lax.dot_general(
                 left[s, j : j + WIDTH, 0:96], right[t, :, half * WIDTH : (half + 1) * WIDTH],
                 (((1,), (0,)), ((), ())), preferred_element_type=F32,
             )
-
-    def fill(k, x, half, factor=None):
+            x[j : j + WIDTH, :] = jnp.maximum(dist, 1e-12)
+
+    def fill(k, x, factor=None):
         for j in range(0, 512, WIDTH):
-            k[j : j + WIDTH, half * WIDTH : (half + 1) * WIDTH] = entries(x[j : j + WIDTH, :], factor)
-
-    def to_t(k, s, t):
-        acc[NS + t] += lax.dot_general(dir_s[s], k[...], (((1,), (0,)), ((), ())), preferred_element_type=F32)
-
-    def to_s(k, s, t):
+            k[j : j + WIDTH, :] = entries(x[j : j + WIDTH, :], factor)
+
+    def to_t(half, s, t):
+        acc[NS + t, :, half * WIDTH : (half + 1) * WIDTH] += lax.dot_general(
+            dir_s[s], (k0, k1)[half][...], (((1,), (0,)), ((), ())), preferred_element_type=F32
+        )
+
+    def to_s(half, s, t):
         acc[s] += lax.dot_general(
-            blk[NS + t, 16:80, :], k[...], (((1,), (1,)), ((), ())), preferred_element_type=F32
+            blk[NS + t, 16:80, half * WIDTH : (half + 1) * WIDTH], (k0, k1)[half][...],
+            (((1,), (1,)), ((), ())), preferred_element_type=F32,
         )
 
     acc[...] = jnp.zeros_like(acc)
-    k1[...] = jnp.zeros_like(k1)
     dir_s[NS] = jnp.zeros_like(dir_s[NS])
     prepare_s(0)
     prepare_t(0)
     cross(x0, 0, 0, 0)
     cross(x1, 0, 0, 1)
-    fill(k0, x0, 0, FACTOR)
-    fill(k0, x1, 1, FACTOR)
-    to_s(k0, 0, 0)
+    fill(k0, x0, FACTOR)
+    fill(k1, x1, FACTOR)
+    to_s(0, 0, 0)
+    to_s(1, 0, 0)
     acc[0] = acc[0] * (1.0 / FACTOR)
+    k1[...] = jnp.zeros_like(k1)
 
     pl.semaphore_wait(barrier, NS - 1 + NG - 1)
-    for s in (4, 1, 3, 2):
+    for s in (4, 1, 3):
         s_copy(s).start()
-    for t in (4, 5, 6):
-        t_copy(t, plane[NG - t]).start()
+    t_copy(4, plane[NG - 4]).start()
 
 
     def plan(q):
         late = q > 8
-        t = jnp.where(late, lax.rem(lax.max(q - 9, 0) + 4, 7) + 1, lax.rem(q + 2, 7) + 1)
+        t = lax.rem(jnp.where(late, 2 * q + 1, 5 * q + 5), 7) + 1
         t = jnp.where(q == 8, 8, t)
         base = jnp.where(q == 8, 1, jnp.where(late, HALF, 0))
         slots = [base, base + 1, base + 2, base + 3]
         return t, slots, slots[0:3] + [jnp.where(q == 8, NS, base + 3)]
 
-    ks = (k0, k1)
-
-    def slot_step(i, now, old, following):
-        (s, t), (old_s, old_dir, old_t) = now, old
+    def block(now, old, following):
+        (s, dir_of, t), (old_s, old_dir, old_t) = now, old
+        to_t(1, old_dir, old_t)
         cross(x1, s, t, 1)
-        to_t(ks[1 - i % 2], old_dir, old_t)
-        fill(ks[i % 2], x0, 0)
+        to_s(1, old_s, old_t)
+        fill(k0, x0)
+        to_t(0, dir_of, t)
         if following is not None:
             cross(x0, following[0], following[1], 0)
-        to_s(ks[1 - i % 2], old_s, old_t)
-        fill(ks[i % 2], x1, 1)
+        to_s(0, s, t)
+        fill(k1, x1)
 
     def strip(q, carry):
         t, slots, dirs = plan(q)
@@ -197,7 +200,7 @@
 
         @pl.when(q < 4)
         def _():
-            later = lax.rem(q + 6, 7) + 1
+            later = lax.rem(5 * q + 4, 7) + 1
             t_copy(later, across(NG - later)).start()
 
         @pl.when(q == 1)
@@ -220,7 +223,7 @@
         old = (before_slots[3], before_dirs[3], before_t)
         for i in range(4):
             following = (after_slots[0], after_t) if i == 3 else (slots[i + 1], t)
-            slot_step(i, (slots[i], t), old, following)
+            block((slots[i], dirs[i], t), old, following)
             old = (slots[i], dirs[i], t)
 
         @pl.when(q == 9)
@@ -248,6 +251,8 @@
     for i, s in enumerate(order):
         if i == 0:
             s_copy(s).wait_recv()
+            s_copy(2).start()
+            t_copy(2, plane[NG - 2]).start()
             prepare_s(s)
             cross(x0, s, 0, 0)
         if i < 3:
@@ -258,34 +263,38 @@
             t_copy(4).wait_recv()
             prepare_t(4)
             following = (0, 4)
-        slot_step(i, (s, 0), old, following)
-        old = (s, NS if s == HALF else s, 0)
-    t_copy(7, plane[NG - 7]).start()
+        if i == 1:
+            t_copy(7, plane[NG - 7]).start()
+        now = (s, NS if s == HALF else s, 0)
+        block(now, old, following)
+        old = now
+    t_copy(5, plane[NG - 5]).start()
     lax.fori_loop(1, 14, strip, 0)
-    order = [(s, t) for s in (5, 6, 7, 4) for t in (3, 4)]
-    old = (7, 7, 2)
+    order = [(s, t) for s in (5, 6, 7, 4) for t in (2, 4)]
+    old = (7, 7, 7)
     for i, (s, t) in enumerate(order):
-        slot_step(i, (s, t), old, order[i + 1] if i < 7 else None)
+        block((s, s, t), old, order[i + 1] if i < 7 else None)
         if i == 0:
-            send_t(2, plane[2])
+            send_t(7, plane[7])
         elif i % 2 == 0:
             send_s(order[i - 1][0])
         old = (s, s, t)
-    send_t(3, plane[3])
-    to_t(k1, 4, 4)
+    send_t(2, plane[2])
+    to_t(1, 4, 4)
     send_t(4, plane[4])
-    to_s(k1, 4, 4)
+    to_s(1, 4, 4)
     send_s(4)
     cross(x0, 0, 8, 0)
     cross(x1, 0, 8, 1)
-    fill(k0, x0, 0)
-    fill(k0, x1, 1)
-    to_s(k0, 0, 8)
+    fill(k0, x0)
+    fill(k1, x1)
+    to_s(0, 0, 8)
+    to_s(1, 0, 8)
 
     loads[3].wait()
     res, dirn = residual[...], direction[...]
     total = acc[0] + acc[NS]
-    for slot in (0, 1, 2, 14, 11, 12, 13, 7, 8, 4, 5, 6, 9, 3, 10):
+    for slot in (0, 1, 2, 14, 12, 7, 9, 11, 13, 4, 5, 6, 8, 3, 10):
         out_copy(slot).wait_recv()
         total = total + got[slot].astype(F32)
     image = total * FACTOR + dirn
@@ -326,7 +335,8 @@
     alpha = norm_old / curv
     fresh = jnp.maximum(norm_old - alpha * (2.0 * mixed - alpha * norm_image), 0.0)
     beta = fresh / norm_old
-    coef_ref[...] = jnp.where(lane == 0, alpha, jnp.where(lane == 1, beta, 0.0))
+    alpha_ref[...] = jnp.broadcast_to(alpha, (64, 512))
+    beta_ref[...] = jnp.broadcast_to(beta, (64, 512))
 
     for s in range(1, NS):
         s_copy(s).wait_send()
@@ -343,11 +353,12 @@
     probes, points = direction.shape
     feats = coords.shape[0]
     dma = pltpu.SemaphoreType.DMA
-    image, coef = pl.pallas_call(
+    big = jax.ShapeDtypeStruct((probes, points), F32)
+    image, alpha, beta = pl.pallas_call(
         kernel,
-        out_shape=(jax.ShapeDtypeStruct((probes, points), F32), jax.ShapeDtypeStruct((probes, 128), F32)),
+        out_shape=(big, big, big),
         in_specs=[pl.BlockSpec(memory_space=pl.ANY)] * 4,
-        out_specs=[pl.BlockSpec(memory_space=pltpu.VMEM)] * 2,
+        out_specs=[pl.BlockSpec(memory_space=pltpu.VMEM)] * 3,
         scratch_shapes=[
             pltpu.VMEM((feats, points), F32),
             pltpu.VMEM((1, feats), F32),
@@ -362,8 +373,8 @@
             pltpu.VMEM((15, 64, 512), BF16),
             pltpu.VMEM((512, WIDTH), F32),
             pltpu.VMEM((512, WIDTH), F32),
-            pltpu.VMEM((512, 512), BF16),
-            pltpu.VMEM((512, 512), BF16),
+            pltpu.VMEM((512, WIDTH), BF16),
+            pltpu.VMEM((512, WIDTH), BF16),
             pltpu.VMEM((8, 128), F32),
             pltpu.VMEM((NS, 8, 128), F32),
             pltpu.VMEM((NG, 8, 128), F32),
@@ -373,7 +384,6 @@
             collective_id=0, has_side_effects=True, vmem_limit_bytes=VMEM
         ),
     )(coords, lengthscale[None, :], residual, direction)
-    alpha, beta = coef[:, 0:1], coef[:, 1:2]
     new_residual = residual - alpha * image
     return solution + alpha * direction, new_residual, new_residual + beta * direction
 

time: 65.8 us -> 61.7 us (0.938)
  Pallas kernels: 61.9 us -> 58.7 us
  local copies, waits for them, and re-layouts: 1.02 us -> 0.01 us
    pallas_call x1, Pallas kernels: 61.9 us -> 58.7 us  [local(): pl.pallas_call(kernel, out_shape=(big, big, big), in_specs=[pl.BlockSpec(...]
    slice x1 -> x0, local copies, waits for them, and re-layouts: 1.01 us -> none  [local(): alpha, beta = (coef[:, 0:1], coef[:, 1:2])]
where the time goes in v4:
time: 61.7 us; the launch traced here: 61.3 us
  Pallas kernels  58.7 us (95%)
  other arithmetic  1.89 us (3%)
  between operations  0.67 us (1%)
    pallas_call x1, Pallas kernels, local(): pl.pallas_call(kernel, out_shape=(big, big, big), in_specs=[pl.BlockSpec(...  58.7 us
    add x1, other arithmetic, local(): new_residual + beta * direction  1.89 us

profile of v4, /device:TPU:1, one launch (start us, length us, event | category | flops | bytes accessed | tf_op | source)
XLA Modules:
  0.0 61.3 jit_solution(1212680542946943598)
XLA Ops:
  0.6 0.0 copy-start
  0.6 0.0 copy-start.1
  0.7 58.7 %shard_map.76 = (f32[64,512]{1,0:T(8,128)}, f32[64,512]{1,0:T(8,128)}, f32[64,512]{1,0:T(8,128)}) custom-call(f32[16,512]{1,0:T(8,128)} %coords_hbm.1, f32[1,16]{1,0:T(1,128)} %bitcast.1, f32[64,512]{1,0:T(8,128)} %residual_hbm.1, f32[64,512]{1,0:T(8,128)} %direction_hbm.1), custom_call_target="tpu_custom_call" | custom-call | tf_op jit(solution)/shard_map/pallas_call | solution.py:357
  59.4 0.0 copy-done
  59.4 0.0 copy-done.1
  59.4 1.9 %multiply_add_fusion = (f32[64,512]{1,0:T(8,128)}, f32[64,512]{1,0:T(8,128)}, f32[64,512]{1,0:T(8,128)}) fusion(f32[64,512]{1,0:T(8,128)} %get-tuple-element.8, f32[64,512]{1,0:T(8,128)S(1)} %copy-done.1, f32[64,512]{1,0:T(8,128)S(1)} %copy-done, f32[64,512]{1,0:T(8,128)} %get-tuple-element.6, f32[64,512]{1,0:T(8,128)} %get-tuple-element.7, f32[64,512]{1,0:T(8,128)} %param.7), kind=kLoop, calls=%fused_computation | loop fusion | flops 196608 | bytes 1179648 | tf_op jit(solution)/shard_map/add | solution.py:388
Async XLA Ops:
  0.6 58.8 %copy-start = (f32[64,512]{1,0:T(8,128)S(1)}, f32[64,512]{1,0:T(8,128)}, u32[]{:S(2)}) copy-start(f32[64,512]{1,0:T(8,128)} %residual_hbm.1) | copy-start | bytes 393220
  0.6 58.8 %copy-start.1 = (f32[64,512]{1,0:T(8,128)S(1)}, f32[64,512]{1,0:T(8,128)}, u32[]{:S(2)}) copy-start(f32[64,512]{1,0:T(8,128)} %direction_hbm.1) | copy-start | bytes 393220

commit v5 on v4

--- a/solution.py
+++ b/solution.py
@@ -139,29 +139,29 @@
             dir_s[s], (k0, k1)[half][...], (((1,), (0,)), ((), ())), preferred_element_type=F32
         )
 
-    def to_s(half, s, t):
-        acc[s] += lax.dot_general(
+    def side_s(half, t):
+        return lax.dot_general(
             blk[NS + t, 16:80, half * WIDTH : (half + 1) * WIDTH], (k0, k1)[half][...],
             (((1,), (1,)), ((), ())), preferred_element_type=F32,
         )
 
+    def to_s(half, s, t):
+        acc[s] += side_s(half, t)
+
     acc[...] = jnp.zeros_like(acc)
+    k1[...] = jnp.zeros_like(k1)
     dir_s[NS] = jnp.zeros_like(dir_s[NS])
     prepare_s(0)
     prepare_t(0)
-    cross(x0, 0, 0, 0)
-    cross(x1, 0, 0, 1)
-    fill(k0, x0, FACTOR)
-    fill(k1, x1, FACTOR)
-    to_s(0, 0, 0)
-    to_s(1, 0, 0)
-    acc[0] = acc[0] * (1.0 / FACTOR)
-    k1[...] = jnp.zeros_like(k1)
 
     pl.semaphore_wait(barrier, NS - 1 + NG - 1)
     for s in (4, 1, 3):
         s_copy(s).start()
-    t_copy(4, plane[NG - 4]).start()
+    for t in (4, 2):
+        t_copy(t, plane[NG - t]).start()
+    s_copy(2).start()
+    for t in (7, 5, 3, 1, 6, 8):
+        t_copy(t, plane[NG - t]).start()
 
 
     def plan(q):
@@ -198,19 +198,12 @@
             t_copy(after_t).wait_recv()
             prepare_t(after_t)
 
-        @pl.when(q < 4)
-        def _():
-            later = lax.rem(5 * q + 4, 7) + 1
-            t_copy(later, across(NG - later)).start()
 
         @pl.when(q == 1)
         def _():
             for s in (5, 7, 6):
                 s_copy(s).start()
 
-        @pl.when(q == 4)
-        def _():
-            t_copy(8, plane[8]).start()
 
         @pl.when(q == 7)
         def _():
@@ -249,13 +242,13 @@
     old = (1, NS, 0)
     order = (4, 1, 3, 2)
     for i, s in enumerate(order):
-        if i == 0:
+        if i < 2:
             s_copy(s).wait_recv()
-            s_copy(2).start()
-            t_copy(2, plane[NG - 2]).start()
             prepare_s(s)
             cross(x0, s, 0, 0)
-        if i < 3:
+        if i == 0:
+            following = None
+        elif i < 3:
             s_copy(order[i + 1]).wait_recv()
             prepare_s(order[i + 1])
             following = (order[i + 1], 0)
@@ -263,12 +256,9 @@
             t_copy(4).wait_recv()
             prepare_t(4)
             following = (0, 4)
-        if i == 1:
-            t_copy(7, plane[NG - 7]).start()
         now = (s, NS if s == HALF else s, 0)
         block(now, old, following)
         old = now
-    t_copy(5, plane[NG - 5]).start()
     lax.fori_loop(1, 14, strip, 0)
     order = [(s, t) for s in (5, 6, 7, 4) for t in (2, 4)]
     old = (7, 7, 7)
@@ -288,12 +278,17 @@
     cross(x1, 0, 8, 1)
     fill(k0, x0)
     fill(k1, x1)
+    cross(x0, 0, 0, 0)
+    cross(x1, 0, 0, 1)
     to_s(0, 0, 8)
     to_s(1, 0, 8)
+    fill(k0, x0, FACTOR)
+    fill(k1, x1, FACTOR)
+    own = side_s(0, 0) + side_s(1, 0)
 
     loads[3].wait()
     res, dirn = residual[...], direction[...]
-    total = acc[0] + acc[NS]
+    total = acc[0] + acc[NS] + own * (1.0 / FACTOR)
     for slot in (0, 1, 2, 14, 12, 7, 9, 11, 13, 4, 5, 6, 8, 3, 10):
         out_copy(slot).wait_recv()
         total = total + got[slot].astype(F32)
@@ -318,6 +313,12 @@
 
     for s in range(1, NS):
         one_copy(s).start()
+    for s in range(1, NS):
+        s_copy(s).wait_send()
+    for t in range(1, NT + 1):
+        t_copy(t).wait_send()
+    for slot in range(15):
+        out_copy(slot).wait_send()
     value = mine[...]
     for s in range(1, NS):
         one_copy(s).wait_recv()
@@ -325,6 +326,8 @@
     two[0] = value
     for t in range(1, NG):
         two_copy(t).start()
+    for s in range(1, NS):
+        one_copy(s).wait_send()
     for t in range(1, NG):
         two_copy(t).wait_recv()
         value = value + two[t]
@@ -338,13 +341,6 @@
     alpha_ref[...] = jnp.broadcast_to(alpha, (64, 512))
     beta_ref[...] = jnp.broadcast_to(beta, (64, 512))
 
-    for s in range(1, NS):
-        s_copy(s).wait_send()
-        one_copy(s).wait_send()
-    for t in range(1, NT + 1):
-        t_copy(t).wait_send()
-    for slot in range(15):
-        out_copy(slot).wait_send()
     for t in range(1, NG):
         two_copy(t).wait_send()
 

time: 61.7 us -> 59.9 us (0.971)
  Pallas kernels: 58.7 us -> 57.2 us
    pallas_call x1, Pallas kernels: 58.7 us -> 57.2 us  [local(): pl.pallas_call(kernel, out_shape=(big, big, big), in_specs=[pl.BlockSpec(...]
where the time goes in v5:
time: 59.9 us; the launch traced here: 59.8 us
  Pallas kernels  57.2 us (95%)
  other arithmetic  1.89 us (3%)
  between operations  0.67 us (1%)
    pallas_call x1, Pallas kernels, local(): pl.pallas_call(kernel, out_shape=(big, big, big), in_specs=[pl.BlockSpec(...  57.2 us
    add x1, other arithmetic, local(): new_residual + beta * direction  1.89 us

profile of v5, /device:TPU:1, one launch (start us, length us, event | category | flops | bytes accessed | tf_op | source)
XLA Modules:
  0.0 59.8 jit_solution(12705019762769652791)
XLA Ops:
  0.6 0.0 copy-start
  0.6 0.0 copy-start.1
  0.7 57.2 %shard_map.76 = (f32[64,512]{1,0:T(8,128)}, f32[64,512]{1,0:T(8,128)}, f32[64,512]{1,0:T(8,128)}) custom-call(f32[16,512]{1,0:T(8,128)} %coords_hbm.1, f32[1,16]{1,0:T(1,128)} %bitcast.1, f32[64,512]{1,0:T(8,128)} %residual_hbm.1, f32[64,512]{1,0:T(8,128)} %direction_hbm.1), custom_call_target="tpu_custom_call" | custom-call | tf_op jit(solution)/shard_map/pallas_call | solution.py:353
  57.8 0.0 copy-done
  57.9 0.0 copy-done.1
  57.9 1.9 %multiply_add_fusion = (f32[64,512]{1,0:T(8,128)}, f32[64,512]{1,0:T(8,128)}, f32[64,512]{1,0:T(8,128)}) fusion(f32[64,512]{1,0:T(8,128)} %get-tuple-element.8, f32[64,512]{1,0:T(8,128)S(1)} %copy-done.1, f32[64,512]{1,0:T(8,128)S(1)} %copy-done, f32[64,512]{1,0:T(8,128)} %get-tuple-element.6, f32[64,512]{1,0:T(8,128)} %get-tuple-element.7, f32[64,512]{1,0:T(8,128)} %param.7), kind=kLoop, calls=%fused_computation | loop fusion | flops 196608 | bytes 1179648 | tf_op jit(solution)/shard_map/add | solution.py:384
Async XLA Ops:
  0.6 57.2 %copy-start = (f32[64,512]{1,0:T(8,128)S(1)}, f32[64,512]{1,0:T(8,128)}, u32[]{:S(2)}) copy-start(f32[64,512]{1,0:T(8,128)} %residual_hbm.1) | copy-start | bytes 393220
  0.6 57.2 %copy-start.1 = (f32[64,512]{1,0:T(8,128)S(1)}, f32[64,512]{1,0:T(8,128)}, u32[]{:S(2)}) copy-start(f32[64,512]{1,0:T(8,128)} %direction_hbm.1) | copy-start | bytes 393220

commit v6 on v5

--- a/solution.py
+++ b/solution.py
@@ -98,62 +98,6 @@
     column = jnp.sum(jnp.where(eye, jnp.broadcast_to(scale[...], (16, 16)), 0.0), axis=1, keepdims=True)
     blk[0, 0:16, :] = (coords[...] / column).astype(BF16)
     blk[0, 16:80, :] = direction[...].astype(BF16)
-    blk[NS] = blk[0]
-
-    def features(slot):
-        wide = blk[slot, 0:16, :].astype(F32)
-        high, mid, low = pieces(jnp.sum(wide * wide, axis=0, keepdims=True))
-        rows = lax.broadcasted_iota(jnp.int32, (8, 512), 0)
-        norm = jnp.where(rows == 0, high, jnp.where(rows == 1, mid, jnp.where(rows == 2, low, 0.0)))
-        return wide, norm, jnp.where(rows < 3, 1.0, 0.0)
-
-    def prepare_s(s):
-        wide, norm, ones = features(s)
-        one_set = jnp.concatenate([wide, norm, ones], axis=0)
-        four = jnp.concatenate([one_set, one_set, one_set, jnp.zeros_like(one_set)], axis=0)
-        left[s] = four.T.astype(BF16)
-        dir_s[s] = blk[s, 16:80, :]
-
-    def prepare_t(t):
-        wide, norm, ones = features(NS + t)
-        turned = jnp.concatenate([wide * (-2.0 * SCALE), ones * SCALE, norm * SCALE], axis=0)
-        high, mid, low = pieces(turned)
-        right[t, 0:32, :] = high.astype(BF16)
-        right[t, 32:64, :] = mid.astype(BF16)
-        right[t, 64:96, :] = low.astype(BF16)
-
-    def cross(x, s, t, half):
-        for j in range(0, 512, WIDTH):
-            dist = lax.dot_general(
-                left[s, j : j + WIDTH, 0:96], right[t, :, half * WIDTH : (half + 1) * WIDTH],
-                (((1,), (0,)), ((), ())), preferred_element_type=F32,
-            )
-            x[j : j + WIDTH, :] = jnp.maximum(dist, 1e-12)
-
-    def fill(k, x, factor=None):
-        for j in range(0, 512, WIDTH):
-            k[j : j + WIDTH, :] = entries(x[j : j + WIDTH, :], factor)
-
-    def to_t(half, s, t):
-        acc[NS + t, :, half * WIDTH : (half + 1) * WIDTH] += lax.dot_general(
-            dir_s[s], (k0, k1)[half][...], (((1,), (0,)), ((), ())), preferred_element_type=F32
-        )
-
-    def side_s(half, t):
-        return lax.dot_general(
-            blk[NS + t, 16:80, half * WIDTH : (half + 1) * WIDTH], (k0, k1)[half][...],
-            (((1,), (1,)), ((), ())), preferred_element_type=F32,
-        )
-
-    def to_s(half, s, t):
-        acc[s] += side_s(half, t)
-
-    acc[...] = jnp.zeros_like(acc)
-    k1[...] = jnp.zeros_like(k1)
-    dir_s[NS] = jnp.zeros_like(dir_s[NS])
-    prepare_s(0)
-    prepare_t(0)
-
     pl.semaphore_wait(barrier, NS - 1 + NG - 1)
     for s in (4, 1, 3):
         s_copy(s).start()
@@ -162,7 +106,63 @@
     s_copy(2).start()
     for t in (7, 5, 3, 1, 6, 8):
         t_copy(t, plane[NG - t]).start()
-
+    for s in (5, 7, 6):
+        s_copy(s).start()
+    blk[NS] = blk[0]
+
+    def features(slot):
+        wide = blk[slot, 0:16, :].astype(F32)
+        high, mid, low = pieces(jnp.sum(wide * wide, axis=0, keepdims=True))
+        rows = lax.broadcasted_iota(jnp.int32, (8, 512), 0)
+        norm = jnp.where(rows == 0, high, jnp.where(rows == 1, mid, jnp.where(rows == 2, low, 0.0)))
+        return wide, norm, jnp.where(rows < 3, 1.0, 0.0)
+
+    def prepare_s(s):
+        wide, norm, ones = features(s)
+        one_set = jnp.concatenate([wide, norm, ones], axis=0)
+        four = jnp.concatenate([one_set, one_set, one_set, jnp.zeros_like(one_set)], axis=0)
+        left[s] = four.T.astype(BF16)
+        dir_s[s] = blk[s, 16:80, :]
+
+    def prepare_t(t):
+        wide, norm, ones = features(NS + t)
+        turned = jnp.concatenate([wide * (-2.0 * SCALE), ones * SCALE, norm * SCALE], axis=0)
+        high, mid, low = pieces(turned)
+        right[t, 0:32, :] = high.astype(BF16)
+        right[t, 32:64, :] = mid.astype(BF16)
+        right[t, 64:96, :] = low.astype(BF16)
+
+    def cross(x, s, t, half):
+        for j in range(0, 512, WIDTH):
+            dist = lax.dot_general(
+                left[s, j : j + WIDTH, 0:96], right[t, :, half * WIDTH : (half + 1) * WIDTH],
+                (((1,), (0,)), ((), ())), preferred_element_type=F32,
+            )
+            x[j : j + WIDTH, :] = jnp.maximum(dist, 1e-12)
+
+    def fill(k, x, factor=None):
+        for j in range(0, 512, WIDTH):
+            k[j : j + WIDTH, :] = entries(x[j : j + WIDTH, :], factor)
+
+    def to_t(half, s, t):
+        acc[NS + t, :, half * WIDTH : (half + 1) * WIDTH] += lax.dot_general(
+            dir_s[s], (k0, k1)[half][...], (((1,), (0,)), ((), ())), preferred_element_type=F32
+        )
+
+    def side_s(half, t):
+        return lax.dot_general(
+            blk[NS + t, 16:80, half * WIDTH : (half + 1) * WIDTH], (k0, k1)[half][...],
+            (((1,), (1,)), ((), ())), preferred_element_type=F32,
+        )
+
+    def to_s(half, s, t):
+        acc[s] += side_s(half, t)
+
+    acc[...] = jnp.zeros_like(acc)
+    k1[...] = jnp.zeros_like(k1)
+    dir_s[NS] = jnp.zeros_like(dir_s[NS])
+    prepare_s(0)
+    prepare_t(0)
 
     def plan(q):
         late = q > 8
@@ -184,26 +184,18 @@
         to_s(0, s, t)
         fill(k1, x1)
 
-    def strip(q, carry):
-        t, slots, dirs = plan(q)
+    def pair(p, carry):
+        q = 2 * p + 1
+        plans = [plan(q), plan(q + 1)]
         before_t, before_slots, before_dirs = plan(q - 1)
         before_t = jnp.where(q == 1, 0, before_t)
-        before_slots = before_slots[0:3] + [jnp.where(q == 1, 2, before_slots[3])]
-        before_dirs = before_dirs[0:3] + [jnp.where(q == 1, 2, before_dirs[3])]
-        after_t, after_slots, _ = plan(q + 1)
-        after_slots = [jnp.where(q == 13, 5, after_slots[0])]
+        after_t, after_slots, _ = plan(q + 2)
 
         @pl.when(q < 7)
         def _():
-            t_copy(after_t).wait_recv()
-            prepare_t(after_t)
-
-
-        @pl.when(q == 1)
-        def _():
-            for s in (5, 7, 6):
-                s_copy(s).start()
-
+            for t in (plans[1][0], after_t):
+                t_copy(t).wait_recv()
+                prepare_t(t)
 
         @pl.when(q == 7)
         def _():
@@ -213,11 +205,14 @@
                 s_copy(s).wait_recv()
                 prepare_s(s)
 
-        old = (before_slots[3], before_dirs[3], before_t)
-        for i in range(4):
-            following = (after_slots[0], after_t) if i == 3 else (slots[i + 1], t)
-            block((slots[i], dirs[i], t), old, following)
-            old = (slots[i], dirs[i], t)
+        old = (
+            jnp.where(q == 1, 2, before_slots[3]), jnp.where(q == 1, 2, before_dirs[3]), before_t,
+        )
+        steps = [(plans[i // 4][1][i % 4], plans[i // 4][2][i % 4], plans[i // 4][0]) for i in range(8)]
+        for i, now in enumerate(steps):
+            following = (steps[i + 1][0], steps[i + 1][2]) if i < 7 else (jnp.where(q == 13, 5, after_slots[0]), after_t)
+            block(now, old, following)
+            old = now
 
         @pl.when(q == 9)
         def _():
@@ -228,6 +223,10 @@
         @pl.when(q > 9)
         def _():
             send_t(before_t, across(before_t))
+
+        @pl.when(q > 8)
+        def _():
+            send_t(plans[0][0], across(plans[0][0]))
 
         return carry
 
@@ -259,17 +258,16 @@
         now = (s, NS if s == HALF else s, 0)
         block(now, old, following)
         old = now
-    lax.fori_loop(1, 14, strip, 0)
-    order = [(s, t) for s in (5, 6, 7, 4) for t in (2, 4)]
-    old = (7, 7, 7)
-    for i, (s, t) in enumerate(order):
-        block((s, s, t), old, order[i + 1] if i < 7 else None)
+    lax.fori_loop(0, 7, pair, 0)
+    order = (5, 6, 7, 4)
+    old = (7, 7, 2)
+    for i, s in enumerate(order):
+        block((s, s, 4), old, (order[i + 1], 4) if i < 3 else None)
         if i == 0:
-            send_t(7, plane[7])
-        elif i % 2 == 0:
-            send_s(order[i - 1][0])
-        old = (s, s, t)
-    send_t(2, plane[2])
+            send_t(2, plane[2])
+        else:
+            send_s(order[i - 1])
+        old = (s, s, 4)
     to_t(1, 4, 4)
     send_t(4, plane[4])
     to_s(1, 4, 4)
@@ -289,7 +287,7 @@
     loads[3].wait()
     res, dirn = residual[...], direction[...]
     total = acc[0] + acc[NS] + own * (1.0 / FACTOR)
-    for slot in (0, 1, 2, 14, 12, 7, 9, 11, 13, 4, 5, 6, 8, 3, 10):
+    for slot in (0, 1, 2, 14, 12, 7, 9, 11, 13, 8, 4, 5, 6, 3, 10):
         out_copy(slot).wait_recv()
         total = total + got[slot].astype(F32)
     image = total * FACTOR + dirn

time: 59.9 us -> 59.7 us (level)
  no operation moved by 1% of the time
where the time goes in v6:
time: 59.7 us; the launch traced here: 59.6 us
  Pallas kernels  57 us (95%)
  other arithmetic  1.89 us (3%)
  between operations  0.67 us (1%)
    pallas_call x1, Pallas kernels, local(): pl.pallas_call(kernel, out_shape=(big, big, big), in_specs=[pl.BlockSpec(...  57 us
    add x1, other arithmetic, local(): new_residual + beta * direction  1.89 us

profile of v6, /device:TPU:1, one launch (start us, length us, event | category | flops | bytes accessed | tf_op | source)
XLA Modules:
  0.0 59.6 jit_solution(16371961057952202793)
XLA Ops:
  0.6 0.0 copy-start
  0.6 0.0 copy-start.1
  0.7 57.0 %shard_map.76 = (f32[64,512]{1,0:T(8,128)}, f32[64,512]{1,0:T(8,128)}, f32[64,512]{1,0:T(8,128)}) custom-call(f32[16,512]{1,0:T(8,128)} %coords_hbm.1, f32[1,16]{1,0:T(1,128)} %bitcast.1, f32[64,512]{1,0:T(8,128)} %residual_hbm.1, f32[64,512]{1,0:T(8,128)} %direction_hbm.1), custom_call_target="tpu_custom_call" | custom-call | tf_op jit(solution)/shard_map/pallas_call | solution.py:351
  57.7 0.0 copy-done
  57.7 0.0 copy-done.1
  57.7 1.9 %multiply_add_fusion = (f32[64,512]{1,0:T(8,128)}, f32[64,512]{1,0:T(8,128)}, f32[64,512]{1,0:T(8,128)}) fusion(f32[64,512]{1,0:T(8,128)} %get-tuple-element.8, f32[64,512]{1,0:T(8,128)S(1)} %copy-done.1, f32[64,512]{1,0:T(8,128)S(1)} %copy-done, f32[64,512]{1,0:T(8,128)} %get-tuple-element.6, f32[64,512]{1,0:T(8,128)} %get-tuple-element.7, f32[64,512]{1,0:T(8,128)} %param.7), kind=kLoop, calls=%fused_computation | loop fusion | flops 196608 | bytes 1179648 | tf_op jit(solution)/shard_map/add | solution.py:382
Async XLA Ops:
  0.6 57.0 %copy-start = (f32[64,512]{1,0:T(8,128)S(1)}, f32[64,512]{1,0:T(8,128)}, u32[]{:S(2)}) copy-start(f32[64,512]{1,0:T(8,128)} %residual_hbm.1) | copy-start | bytes 393220
  0.6 57.0 %copy-start.1 = (f32[64,512]{1,0:T(8,128)S(1)}, f32[64,512]{1,0:T(8,128)}, u32[]{:S(2)}) copy-start(f32[64,512]{1,0:T(8,128)} %direction_hbm.1) | copy-start | bytes 393220
